TPU v7x, 256 devices: a whole 4x4x8 slice. The times are simulated.
256 devices in a mesh: dp: 16 (over z_lo, x, core), ctx: 16 (over z_hi, y).
Axes of the slice: x: 4, y: 4, z: 8 (z_hi: 4, z_lo: 2; z = z_hi * 2 + z_lo), core: 2. Of those that a mesh axis runs over, the one named last changes fastest.
Arguments:
- hidden_rows: bfloat16 [32768, 4096], P(('dp', 'ctx')), may hold values from -6 to 6
- query_rows: bfloat16 [32768, 2048], P(('dp', 'ctx')), may hold values from -17 to 17
- out_grad: bfloat16 [32768, 2048], P(('dp', 'ctx')), may hold values from -6 to 6
- projection: bfloat16 [1024, 4096], replicated, may hold values from -0.09375 to 0.09375
- packing_plan: int32 [256, 128], P(('dp', 'ctx')), may hold values from 0 to 127, each once within a row
- document_ids: int32 [16, 2048], P('dp'), may hold values from 0 to 7, never falling along the last dimension, each value on 1 to 1536 neighbouring positions
Outputs:
- attended: bfloat16 [32768, 2048], P(('dp', 'ctx'))
- query_grad: bfloat16 [32768, 2048], P(('dp', 'ctx'))
- hidden_grad: bfloat16 [32768, 4096], P(('dp', 'ctx'))
- weight_grad: float32 [1024, 4096], P('dp', 'ctx')
Inputs may be any that keep to these rules, and one draw needn't show every extreme that they name: `packing_plan`: each row holds every value once, so each device sends exactly 8 rows to each packed sequence. `document_ids`: never falling along a sequence; a document spans at most 1536 positions, and some document exactly that many.
All inputs are finite; a program needn't handle non-finite values.
Results may differ from a plain program's by a relative error of at most 0.017.
The roundings to bfloat16 on the way count: a program that leaves them out, or rounds other values in their place, can miss the bound.
Values may be sent and summed in bfloat16 or wider, within the bound.
A program may use at most 64 MiB of HBM per device.

v0:
```python
import math

import jax
import jax.numpy as jnp
from jax import lax
from jax.sharding import PartitionSpec as P

KV_HEADS = 4
HEAD_DIM = 128


ROPE_BASE = 500000.0
MASK_VALUE = -1e30


def rotary_tables(positions, head_width):
    half_width = head_width // 2
    exponent = jnp.arange(half_width, dtype=jnp.float32) * (-2.0 * math.log(ROPE_BASE) / head_width)
    angles = positions.astype(jnp.float32)[:, None] * jnp.exp(exponent)[None, :]
    return (jnp.cos(angles), jnp.sin(angles))


def rotate_forward(head_rows, cosine_table, sine_table):
    half_width = head_rows.shape[-1] // 2
    first_half = head_rows[..., :half_width]
    second_half = head_rows[..., half_width:]
    cosine_part = cosine_table[:, None, :]
    sine_part = sine_table[:, None, :]
    return jnp.concatenate(
        [
            first_half * cosine_part - second_half * sine_part,
            second_half * cosine_part + first_half * sine_part,
        ],
        axis=-1,
    )


def rotate_adjoint(head_grads, cosine_table, sine_table):
    half_width = head_grads.shape[-1] // 2
    first_half = head_grads[..., :half_width]
    second_half = head_grads[..., half_width:]
    cosine_part = cosine_table[:, None, :]
    sine_part = sine_table[:, None, :]
    return jnp.concatenate(
        [
            first_half * cosine_part + second_half * sine_part,
            second_half * cosine_part - first_half * sine_part,
        ],
        axis=-1,
    )


def inner_rows(left_side, right_side):
    return lax.dot_general(
        left_side, right_side, (((1,), (1,)), ((), ())), preferred_element_type=jnp.float32
    )


def outer_rows(left_side, right_side):
    return lax.dot_general(
        left_side, right_side, (((0,), (0,)), ((), ())), preferred_element_type=jnp.float32
    )


def block_terms(
    query_block, grad_block, key_rows, value_rows, query_index, query_document, key_document
):
    score_scale = key_rows.shape[1] ** (-0.5)
    scores = inner_rows(query_block, key_rows) * score_scale
    key_index = jnp.arange(key_rows.shape[0], dtype=jnp.int32)
    allowed = (key_index[None, :] <= query_index[:, None]) & (
        key_document[None, :] == query_document[:, None]
    )
    scores = jnp.where(allowed, scores, MASK_VALUE)
    row_max = jnp.max(scores, axis=1, keepdims=True)
    exponent = jnp.exp(scores - row_max)
    probability = exponent / jnp.sum(exponent, axis=1, keepdims=True)
    rounded = probability.astype(jnp.bfloat16)
    attended = jnp.dot(rounded, value_rows, preferred_element_type=jnp.float32).astype(jnp.bfloat16)
    grad_prob = inner_rows(grad_block, value_rows)
    delta_sum = jnp.sum(probability * grad_prob, axis=1, keepdims=True)
    grad_score = (probability * (grad_prob - delta_sum)).astype(jnp.bfloat16)
    query_grad = (
        jnp.dot(grad_score, key_rows, preferred_element_type=jnp.float32) * score_scale
    ).astype(jnp.bfloat16)
    key_part = outer_rows(grad_score, query_block) * score_scale
    value_part = outer_rows(rounded, grad_block)
    return (attended, query_grad, key_part, value_part)


def body(hidden_rows, query_rows, out_grad, projection, packing_plan, document_ids):
    row_count = hidden_rows.shape[0]
    split_size = lax.axis_size("ctx")
    part_index = lax.axis_index("ctx")
    sequences = lax.axis_size("dp")
    order_rows = jnp.argsort(packing_plan[0])
    send_hidden = jnp.take(hidden_rows, order_rows, axis=0)
    send_query = jnp.take(query_rows, order_rows, axis=0)
    packed_hidden, packed_query = (
        lax.all_to_all(send_hidden, "dp", split_axis=0, concat_axis=0, tiled=True),
        lax.all_to_all(send_query, "dp", split_axis=0, concat_axis=0, tiled=True),
    )
    projected = inner_rows(packed_hidden, projection)
    positions = part_index * row_count + jnp.arange(row_count, dtype=jnp.int32)
    cosine_table, sine_table = rotary_tables(positions, HEAD_DIM)
    key_width = KV_HEADS * HEAD_DIM
    key_heads = rotate_forward(
        projected[:, :key_width].reshape(row_count, KV_HEADS, HEAD_DIM), cosine_table, sine_table
    ).astype(jnp.bfloat16)
    values = projected[:, key_width:].reshape(row_count, KV_HEADS, HEAD_DIM).astype(jnp.bfloat16)
    repeats = split_size // KV_HEADS
    group_index = part_index // repeats
    local_query = lax.all_to_all(packed_query, "ctx", split_axis=1, concat_axis=0, tiled=True)
    all_keys, all_values = (
        lax.all_gather(key_heads.reshape(row_count, key_width), "ctx", axis=0, tiled=True),
        lax.all_gather(values.reshape(row_count, key_width), "ctx", axis=0, tiled=True),
    )
    local_keys = lax.dynamic_slice_in_dim(all_keys, group_index * HEAD_DIM, HEAD_DIM, 1)
    local_values = lax.dynamic_slice_in_dim(all_values, group_index * HEAD_DIM, HEAD_DIM, 1)
    local_grad = lax.all_to_all(out_grad, "ctx", split_axis=1, concat_axis=0, tiled=True)
    length = local_query.shape[0]
    block_rows = math.gcd(length, 512)
    block_count = length // block_rows
    documents = document_ids[0]
    starts = jnp.arange(block_count, dtype=jnp.int32) * block_rows
    key_total = jnp.zeros((length, HEAD_DIM), jnp.float32)
    value_total = jnp.zeros((length, HEAD_DIM), jnp.float32)
    query_blocks = local_query.reshape(block_count, block_rows, HEAD_DIM)
    grad_blocks = local_grad.reshape(block_count, block_rows, HEAD_DIM)

    def block_step(carry_pair, inputs):
        query_block, grad_block, block_start = inputs
        query_index = block_start + jnp.arange(block_rows, dtype=jnp.int32)
        query_document = lax.dynamic_slice_in_dim(documents, block_start, block_rows)
        attended_block, query_block_grad, key_part, value_part = block_terms(
            query_block,
            grad_block,
            local_keys,
            local_values,
            query_index,
            query_document,
            documents,
        )
        return (
            (carry_pair[0] + key_part, carry_pair[1] + value_part),
            (attended_block, query_block_grad),
        )

    (key_total, value_total), (attended_blocks, query_grad_blocks) = lax.scan(
        block_step, (key_total, value_total), (query_blocks, grad_blocks, starts)
    )
    attended_parts = attended_blocks.reshape(length, HEAD_DIM)
    query_parts = query_grad_blocks.reshape(length, HEAD_DIM)
    attended = lax.all_to_all(attended_parts, "ctx", split_axis=0, concat_axis=1, tiled=True)
    query_grad = lax.all_to_all(query_parts, "ctx", split_axis=0, concat_axis=1, tiled=True)
    key_slots_grad, value_slots_grad = (
        lax.all_to_all(key_total, "ctx", split_axis=0, concat_axis=1, tiled=True),
        lax.all_to_all(value_total, "ctx", split_axis=0, concat_axis=1, tiled=True),
    )
    key_grad = (
        key_slots_grad.reshape(row_count, KV_HEADS, repeats, HEAD_DIM)
        .sum(axis=2)
        .astype(jnp.bfloat16)
    )
    value_grad = (
        value_slots_grad.reshape(row_count, KV_HEADS, repeats, HEAD_DIM)
        .sum(axis=2)
        .astype(jnp.bfloat16)
    )
    key_back = rotate_adjoint(key_grad.astype(jnp.float32), cosine_table, sine_table).reshape(
        row_count, key_width
    )
    projected_grad = jnp.concatenate(
        [key_back, value_grad.reshape(row_count, key_width).astype(jnp.float32)], axis=1
    ).astype(jnp.bfloat16)
    hidden_grad = jnp.dot(projected_grad, projection, preferred_element_type=jnp.float32).astype(
        jnp.bfloat16
    )
    block_term = outer_rows(projected_grad, packed_hidden)
    partial_sum = lax.psum_scatter(
        block_term.astype(jnp.bfloat16), "ctx", scatter_dimension=1, tiled=True
    ).astype(jnp.float32)
    weight_grad = lax.psum_scatter(partial_sum, "dp", scatter_dimension=0, tiled=True)
    weight_grad = weight_grad / sequences
    return (attended, query_grad, hidden_grad, weight_grad)


def solution(mesh):
    in_specs = (
        P(("dp", "ctx"), None),
        P(("dp", "ctx"), None),
        P(("dp", "ctx"), None),
        P(),
        P(("dp", "ctx"), None),
        P("dp", None),
    )
    out_specs = (
        P(("dp", "ctx"), None),
        P(("dp", "ctx"), None),
        P(("dp", "ctx"), None),
        P("dp", "ctx"),
    )
    return jax.shard_map(body, mesh=mesh, in_specs=in_specs, out_specs=out_specs, check_vma=False)
```

profile of v0, /device:TPU:1, one launch (start us, length us, event | category | flops | bytes accessed | tf_op | source)
XLA Modules:
  0.0 536.7 jit_solution(12122289228077635019)
XLA Ops:
  7.2 3.3 sort.17
  12.9 7.2 %all-to-all-start.2 = ((bf16[16,8,4096]{2,1,0:T(8,128)(2,1)}), bf16[16,8,4096]{2,1,0:T(8,128)(2,1)S(1)}, u32[]{:S(2)}, u32[]{:S(2)}) async-start(bf16[16,8,4096]{2,1,0:T(8,128)(2,1)} %bitcast_select_fusion), calls=%async_computation.2 | async-start | bytes 2097152 | tf_op jit(solution)/shard_map/all_to_all | solution.py:100
  20.5 15.4 %all-to-all-done.2 = bf16[16,8,4096]{2,1,0:T(8,128)(2,1)S(1)} async-done(((bf16[16,8,4096]{2,1,0:T(8,128)(2,1)}), bf16[16,8,4096]{2,1,0:T(8,128)(2,1)S(1)}, u32[]{:S(2)}, u32[]{:S(2)}) %all-to-all-start.2) | async-done | bytes 1048608 | tf_op jit(solution)/shard_map/all_to_all | solution.py:100
  35.9 6.3 %fusion.27 = f32[128,1024]{1,0:T(8,128)S(1)} fusion(bf16[1024,4096]{1,0:T(8,128)(2,1)} %param.11, bf16[16,8,4096]{2,1,0:T(8,128)(2,1)S(1)} %all-to-all-done.2), kind=kOutput, calls=%fused_computation.41 | convolution fusion | flops 1073741824 | bytes 9961472 | tf_op jit(solution)/shard_map/dot_general | solution.py:54
  49.3 4.2 all-to-all-start
  55.5 7.9 %all-to-all-done = bf16[16,8,2048]{2,1,0:T(8,128)(2,1)S(1)} async-done(((bf16[16,8,2048]{2,1,0:T(8,128)(2,1)}), bf16[16,8,2048]{2,1,0:T(8,128)(2,1)S(1)}, u32[]{:S(2)}, u32[]{:S(2)}) %all-to-all-start) | async-done | bytes 524320 | tf_op jit(solution)/shard_map/all_to_all | solution.py:101
  63.4 10.5 %all-to-all-start.3 = ((bf16[128,16,128]{2,0,1:T(8,128)(2,1)}), bf16[128,16,128]{2,0,1:T(8,128)(2,1)S(1)}, u32[]{:S(2)}, u32[]{:S(2)}) async-start(bf16[128,16,128]{2,0,1:T(8,128)(2,1)} %copy_bitcast_fusion), calls=%async_computation.3 | async-start | bytes 1048576 | tf_op jit(solution)/shard_map/all_to_all | solution.py:120
  75.0 14.9 %all-to-all-done.3 = bf16[128,16,128]{2,0,1:T(8,128)(2,1)S(1)} async-done(((bf16[128,16,128]{2,0,1:T(8,128)(2,1)}), bf16[128,16,128]{2,0,1:T(8,128)(2,1)S(1)}, u32[]{:S(2)}, u32[]{:S(2)}) %all-to-all-start.3) | async-done | bytes 524320 | tf_op jit(solution)/shard_map/all_to_all | solution.py:120
  90.0 6.1 %all-to-all-start.1 = ((bf16[128,16,128]{2,0,1:T(8,128)(2,1)}), bf16[128,16,128]{2,0,1:T(8,128)(2,1)}, u32[]{:S(2)}, u32[]{:S(2)}) async-start(bf16[128,16,128]{2,0,1:T(8,128)(2,1)} %copy.22), calls=%async_computation.1 | async-start | bytes 1048576 | tf_op jit(solution)/shard_map/all_to_all | solution.py:113
  96.2 27.6 %all-gather.3.cloned.1.call-done = bf16[2048,512]{0,1:T(8,128)(2,1)} async-done(((bf16[128,512]{0,1:T(8,128)(2,1)}), bf16[2048,512]{0,1:T(8,128)(2,1)}) %all-gather.3.cloned.1.call-update) | async-done | bytes 2097168 | tf_op jit(solution)/shard_map/all_gather | solution.py:115
  127.7 56.8 %all-gather.5.cloned.1.call-done = bf16[2048,512]{1,0:T(8,128)(2,1)} async-done(((bf16[128,512]{1,0:T(8,128)(2,1)}), bf16[2048,512]{1,0:T(8,128)(2,1)}) %all-gather.5.cloned.1.call-update) | async-done | bytes 2097168 | tf_op jit(solution)/shard_map/all_gather | solution.py:116
  186.4 83.6 %while.17 = (s32[]{:T(128)}, f32[2048,128]{1,0:T(8,128)S(1)}, f32[2048,128]{1,0:T(8,128)}, bf16[4,512,128]{2,1,0:T(8,128)(2,1)}, bf16[4,512,128]{2,1,0:T(8,128)(...) while((s32[]{:T(128)}, f32[2048,128]{1,0:T(8,128)S(1)}, ...), condition=%wide.region_5.6_spmd.clone, body=%wide.region_1.5_spmd.clone.sunk | while | flops 1636236288 | bytes 86818136 | solution.py:149
  189.7 2.5 fusion.67
  195.7 4.4 convolution_add_fusion.2
  203.6 2.1 fusion.69
  210.4 2.5 fusion.67
  216.3 4.8 convolution_add_fusion.2
  231.3 2.5 fusion.67
  237.3 4.8 convolution_add_fusion.2
  245.5 2.1 fusion.69
  252.3 2.5 fusion.67
  258.3 4.8 convolution_add_fusion.2
  270.0 27.5 %all_to_all.117 = f32[16,128,128]{2,1,0:T(8,128)} all-to-all(f32[16,128,128]{2,1,0:T(8,128)S(1)} %bitcast.106), channel_id=1, replica_groups=mesh['dp'=16,'ctx'=16] {'ctx'}, dimensions={0} | all-to-all | bytes 2097152 | tf_op jit(solution)/shard_map/all_to_all | solution.py:157
  297.5 6.0 %all-to-all-start.7 = ((f32[16,128,128]{2,1,0:T(8,128)}), f32[16,128,128]{2,1,0:T(8,128)S(1)}, u32[]{:S(2)}, u32[]{:S(2)}) async-start(f32[16,128,128]{2,1,0:T(8,128)} %bitcast.115), calls=%async_computation.7 | async-start | bytes 2097152 | tf_op jit(solution)/shard_map/all_to_all | solution.py:158
  305.3 14.8 %all-to-all-done.7 = f32[16,128,128]{2,1,0:T(8,128)S(1)} async-done(((f32[16,128,128]{2,1,0:T(8,128)}), f32[16,128,128]{2,1,0:T(8,128)S(1)}, u32[]{:S(2)}, u32[]{:S(2)}) %all-to-all-start.7) | async-done | bytes 1048608 | tf_op jit(solution)/shard_map/all_to_all | solution.py:158
  320.3 5.6 %convolution_convert_fusion.1 = bf16[1024,4096]{1,0:T(8,128)(2,1)} fusion(bf16[16,8,4096]{2,1,0:T(8,128)(2,1)S(1)} %all-to-all-done.2, bf16[128,512]{0,1:T(8,128)(2,1)S(1)} %bitcast.113, bf16[128,512]{0,1:T(8,128)(2,1)S(1)} %bitcast.111), kind=kOutput, calls=%fused_computation.36 | convolution fusion | flops 1078460416 | bytes 9699328 | tf_op jit(solution)/shard_map/dot_general | solution.py:60
  325.9 6.1 %all-to-all-start.4 = ((bf16[16,128,128]{2,1,0:T(8,128)(2,1)}), bf16[16,128,128]{2,1,0:T(8,128)(2,1)S(1)}, u32[]{:S(2)}, u32[]{:S(2)}) async-start(bf16[16,128,128]{2,1,0:T(8,128)(2,1)} %bitcast.10), calls=%async_computation.4 | async-start | bytes 1048576 | tf_op jit(solution)/shard_map/all_to_all | solution.py:154
  332.1 130.6 %reduce-scatter.3.cloned.1.call-done = bf16[1024,256]{1,0:T(8,128)(2,1)} async-done(((bf16[1024,4096]{1,0:T(8,128)(2,1)}), bf16[1024,256]{1,0:T(8,128)(2,1)}) %reduce-scatter.3.cloned.1.call-update) | async-done | bytes 524304 | tf_op jit(solution)/shard_map/reduce_scatter | solution.py:180
  464.8 6.8 %all-to-all-start.5 = ((bf16[16,128,128]{2,1,0:T(8,128)(2,1)}), bf16[16,128,128]{2,1,0:T(8,128)(2,1)S(1)}, u32[]{:S(2)}, u32[]{:S(2)}) async-start(bf16[16,128,128]{2,1,0:T(8,128)(2,1)} %bitcast.13), calls=%async_computation.5 | async-start | bytes 1048576 | tf_op jit(solution)/shard_map/all_to_all | solution.py:155
  472.9 11.0 %all-to-all-done.5 = bf16[16,128,128]{2,1,0:T(8,128)(2,1)S(1)} async-done(((bf16[16,128,128]{2,1,0:T(8,128)(2,1)}), bf16[16,128,128]{2,1,0:T(8,128)(2,1)S(1)}, u32[]{:S(2)}, u32[]{:S(2)}) %all-to-all-start.5) | async-done | bytes 524320 | tf_op jit(solution)/shard_map/all_to_all | solution.py:155
  485.1 5.7 %convolution_convert_fusion.2 = bf16[128,4096]{1,0:T(8,128)(2,1)} fusion(bf16[1024,4096]{1,0:T(8,128)(2,1)} %param.11, bf16[128,512]{0,1:T(8,128)(2,1)S(1)} %bitcast.114, bf16[128,512]{0,1:T(8,128)(2,1)S(1)} %bitcast.112), kind=kOutput, calls=%fused_computation.37 | convolution fusion | flops 1074790400 | bytes 9699328 | tf_op jit(solution)/shard_map/dot_general | solution.py:176
  490.8 37.9 %reduce-scatter.5.cloned.1.call-done = f32[64,256]{1,0:T(8,128)} async-done(((f32[1024,256]{1,0:T(8,128)}), f32[64,256]{1,0:T(8,128)}) %reduce-scatter.5.cloned.1.call-update) | async-done | bytes 65552 | tf_op jit(solution)/shard_map/reduce_scatter | solution.py:183
  (135 shorter events, 69.5 us)
Async XLA Ops:
  7.2 3.4 copy-start
  12.9 23.0 %all-to-all-start.2 = ((bf16[16,8,4096]{2,1,0:T(8,128)(2,1)}), bf16[16,8,4096]{2,1,0:T(8,128)(2,1)S(1)}, u32[]{:S(2)}, u32[]{:S(2)}) async-start(bf16[16,8,4096]{2,1,0:T(8,128)(2,1)} %bitcast_select_fusion), calls=%async_computation.2 | async-start | bytes 2097152 | tf_op jit(solution)/shard_map/all_to_all | solution.py:100
  20.1 103.7 %all-gather.3.cloned.1.call-start = ((), (), s32[]{:S(2)}) async-start(), calls=%async_computation.10 | async-start | bytes 2228224 | tf_op jit(solution)/shard_map/all_gather | solution.py:115
  42.2 5.3 copy-start.3
  46.7 137.9 %all-gather.5.cloned.1.call-start = ((), (), s32[]{:S(2)}) async-start(), calls=%async_computation.11 | async-start | bytes 2228224 | tf_op jit(solution)/shard_map/all_gather | solution.py:116
  49.3 14.1 %all-to-all-start = ((bf16[16,8,2048]{2,1,0:T(8,128)(2,1)}), bf16[16,8,2048]{2,1,0:T(8,128)(2,1)S(1)}, u32[]{:S(2)}, u32[]{:S(2)}) async-start(bf16[16,8,2048]{2,1,0:T(8,128)(2,1)} %bitcast_select_fusion.1), calls=%async_computation | async-start | bytes 1048576 | tf_op jit(solution)/shard_map/all_to_all | solution.py:101
  53.5 132.9 %copy-start.8 = (s32[1,2048]{1,0:T(1,128)S(1)}, s32[1,2048]{1,0:T(1,128)}, u32[]{:S(2)}) copy-start(s32[1,2048]{1,0:T(1,128)} %param.13) | copy-start | bytes 24580
  63.4 26.5 %all-to-all-start.3 = ((bf16[128,16,128]{2,0,1:T(8,128)(2,1)}), bf16[128,16,128]{2,0,1:T(8,128)(2,1)S(1)}, u32[]{:S(2)}, u32[]{:S(2)}) async-start(bf16[128,16,128]{2,0,1:T(8,128)(2,1)} %copy_bitcast_fusion), calls=%async_computation.3 | async-start | bytes 1048576 | tf_op jit(solution)/shard_map/all_to_all | solution.py:120
  90.0 6.1 %copy-start.4 = (bf16[128,16,128]{2,0,1:T(8,128)(2,1)}, bf16[128,16,128]{2,0,1:T(8,128)(2,1)S(1)}, u32[]{:S(2)}) copy-start(bf16[128,16,128]{2,0,1:T(8,128)(2,1)S(1)} %all-to-all-done.3) | copy-start | bytes 1572868
  90.0 96.5 %all-to-all-start.1 = ((bf16[128,16,128]{2,0,1:T(8,128)(2,1)}), bf16[128,16,128]{2,0,1:T(8,128)(2,1)}, u32[]{:S(2)}, u32[]{:S(2)}) async-start(bf16[128,16,128]{2,0,1:T(8,128)(2,1)} %copy.22), calls=%async_computation.1 | async-start | bytes 1048576 | tf_op jit(solution)/shard_map/all_to_all | solution.py:113
  189.7 4.5 copy-start.6
  192.2 2.0 copy-start.1
  195.7 4.4 copy-start.2
  195.7 4.4 copy-start.7
  203.6 2.1 copy-start.5
  210.3 4.5 copy-start.6
  216.3 4.8 copy-start.2
  216.3 4.8 copy-start.7
  224.5 2.1 copy-start.5
  231.3 4.5 copy-start.6
  237.3 4.8 copy-start.2
  237.3 4.8 copy-start.7
  245.5 2.1 copy-start.5
  252.3 4.5 copy-start.6
  258.3 4.8 copy-start.2
  258.3 4.8 copy-start.7
  266.5 2.1 copy-start.5
  297.5 22.6 %all-to-all-start.7 = ((f32[16,128,128]{2,1,0:T(8,128)}), f32[16,128,128]{2,1,0:T(8,128)S(1)}, u32[]{:S(2)}, u32[]{:S(2)}) async-start(f32[16,128,128]{2,1,0:T(8,128)} %bitcast.115), calls=%async_computation.7 | async-start | bytes 2097152 | tf_op jit(solution)/shard_map/all_to_all | solution.py:158
  303.5 159.1 %reduce-scatter.3.cloned.1.call-start = ((), (), s32[]{:S(2)}) async-start(), calls=%async_computation.12 | async-start | bytes 8912896 | tf_op jit(solution)/shard_map/reduce_scatter | solution.py:180
  325.9 138.9 %all-to-all-start.4 = ((bf16[16,128,128]{2,1,0:T(8,128)(2,1)}), bf16[16,128,128]{2,1,0:T(8,128)(2,1)S(1)}, u32[]{:S(2)}, u32[]{:S(2)}) async-start(bf16[16,128,128]{2,1,0:T(8,128)(2,1)} %bitcast.10), calls=%async_computation.4 | async-start | bytes 1048576 | tf_op jit(solution)/shard_map/all_to_all | solution.py:154
  332.0 196.6 %reduce-scatter.5.cloned.1.call-start = ((), (), s32[]{:S(2)}) async-start(), calls=%async_computation.13 | async-start | bytes 1114112 | tf_op jit(solution)/shard_map/reduce_scatter | solution.py:183
  464.8 19.1 %all-to-all-start.5 = ((bf16[16,128,128]{2,1,0:T(8,128)(2,1)}), bf16[16,128,128]{2,1,0:T(8,128)(2,1)S(1)}, u32[]{:S(2)}, u32[]{:S(2)}) async-start(bf16[16,128,128]{2,1,0:T(8,128)(2,1)} %bitcast.13), calls=%async_computation.5 | async-start | bytes 1048576 | tf_op jit(solution)/shard_map/all_to_all | solution.py:155
  (3 other events, 5.9 us)
Sparse Core Ops, SparseCore 0:
  46.8 76.8 all-gather.2
  126.2 58.3 all-gather.4
  326.0 136.5 reduce-scatter.2
  465.0 63.6 reduce-scatter.4
where the time goes:
time: 541 us; the launch traced here: 537 us
  waiting for transfers between devices  317 us (59%)
  matrix products  74.6 us (14%)
  starting transfers between devices  47.2 us (9%)
  blocking collectives  27.5 us (5%)
  local copies, waits for them, and re-layouts  25.9 us (5%)
  other arithmetic  22.5 us (4%)
  between operations  14.1 us (3%)
  loops' own time  8.02 us (1%)
    reduce_scatter x1, waiting for transfers between devices, body(): lax.psum_scatter(block_term.astype(jnp.bfloat16), 'ctx', scatter_dimensio...  131 us
    all_gather x1, waiting for transfers between devices, body(): lax.all_gather(values.reshape(row_count, key_width), 'ctx', axis=0, tiled...  56.8 us
    reduce_scatter x1, waiting for transfers between devices, body(): lax.psum_scatter(partial_sum, 'dp', scatter_dimension=0, tiled=True)  37.9 us
    dot_general x9, matrix products, outer_rows(): lax.dot_general(left_side, right_side, (((0,), (0,)), ((), ())), preferre...  32.8 us
    all_gather x1, waiting for transfers between devices, body(): lax.all_gather(key_heads.reshape(row_count, key_width), 'ctx', axis=0, ti...  27.6 us
    all_to_all x1, blocking collectives, body(): lax.all_to_all(key_total, 'ctx', split_axis=0, concat_axis=1, tiled=True)  27.5 us
    dot_general x9, matrix products, inner_rows(): lax.dot_general(left_side, right_side, (((1,), (1,)), ((), ())), preferre...  24.5 us
    all_to_all x1, waiting for transfers between devices, body(): lax.all_to_all(send_hidden, 'dp', split_axis=0, concat_axis=0, tiled=True)  15.4 us
  transfers between devices with their start and end apart: 11, of which 9 were waited for; matrix products, arithmetic and copies ran while one was open for 4% of the time, Pallas kernels for 0%

commit v1 on v0

v1 whole, which is shorter than its diff:
```python
import functools
import math

import jax
import jax.numpy as jnp
from jax import lax
from jax.experimental import pallas as pl
from jax.experimental.pallas import tpu as pltpu
from jax.sharding import PartitionSpec as P

ROPE_BASE = 500000.0
MASK_VALUE = -1e30
HD = 128
SCALE = HD ** (-0.5)
BF = jnp.bfloat16
F32 = jnp.float32
MESH = pl.DeviceIdType.MESH
KB = 256
MIB = 1024 * 1024


def vm():
    return pl.BlockSpec(memory_space=pltpu.VMEM)


def rows_dot(a, b):
    return lax.dot_general(a, b, (((1,), (1,)), ((), ())), preferred_element_type=F32)


def cols_dot(a, b):
    return lax.dot_general(a, b, (((0,), (0,)), ((), ())), preferred_element_type=F32)


def angle_tables(positions):
    half = HD // 2
    exponent = jnp.arange(half, dtype=F32) * (-2.0 * math.log(ROPE_BASE) / HD)
    angles = positions.astype(F32)[:, None] * jnp.exp(exponent)[None, :]
    cosine, sine = jnp.cos(angles), jnp.sin(angles)
    return jnp.concatenate([cosine, cosine], 1), jnp.concatenate([-sine, sine], 1)


def project_kernel(plan, x, q, og, w, cos, sin, kv, qs, gs, hs, xp, acc):
    step = pl.program_id(0)

    @pl.when(step == 0)
    def _():
        pick = (lax.broadcasted_iota(jnp.int32, (128, 128), 0) == plan[...]).astype(F32).astype(BF)
        for j in range(16):
            sl = slice(j * 256, (j + 1) * 256)
            t = jnp.dot(pick, x[:, sl], preferred_element_type=F32).astype(BF)
            xp[:, sl] = t
            hs[j % 4, :, (j // 4) * 256 : (j // 4 + 1) * 256] = t
        for i in range(8):
            parts, grads = [], []
            for h in (2 * i, 2 * i + 1):
                sl = slice(h * HD, (h + 1) * HD)
                parts.append(jnp.dot(pick, q[:, sl], preferred_element_type=F32).reshape(16, 8, HD))
                grads.append(og[:, sl].astype(F32).reshape(16, 8, HD))
            qs[:, i * 16 : (i + 1) * 16, :] = jnp.concatenate(parts, 1).astype(BF)
            gs[i // 2, :, (i % 2) * 16 : (i % 2 + 1) * 16, :] = jnp.concatenate(grads, 1).astype(BF)

    acc[step] = rows_dot(xp[...], w[...])

    @pl.when(step == 3)
    def _():
        for g in range(4):
            sl = slice((g % 2) * HD, (g % 2 + 1) * HD)
            k = acc[g // 2][:, sl]
            v = acc[2 + g // 2][:, sl]
            k3 = k.reshape(16, 8, HD)
            r3 = pltpu.roll(k, 64, 1).reshape(16, 8, HD)
            rot = k3 * cos[...][None] + r3 * sin[...][None]
            kv[:, g * 16 : (g + 1) * 16, :] = jnp.concatenate([rot, v.reshape(16, 8, HD)], 1).astype(BF)


def project(plan, x, q, og, w, cos, sin):
    full = lambda *shape: pl.BlockSpec(shape, lambda i: (0,) * len(shape))
    return pl.pallas_call(
        project_kernel,
        grid=(4,),
        in_specs=[
            full(1, 128), full(128, 4096), full(128, 2048), full(128, 2048),
            pl.BlockSpec((256, 4096), lambda i: (i, 0)), full(8, HD), full(8, HD),
        ],
        out_specs=[full(16, 64, HD), full(16, 128, HD), full(4, 16, 32, HD), full(4, 128, 1024)],
        out_shape=[
            jax.ShapeDtypeStruct((16, 64, HD), BF),
            jax.ShapeDtypeStruct((16, 128, HD), BF),
            jax.ShapeDtypeStruct((4, 16, 32, HD), BF),
            jax.ShapeDtypeStruct((4, 128, 1024), BF),
        ],
        scratch_shapes=[pltpu.VMEM((128, 4096), BF), pltpu.VMEM((4, 128, 256), F32)],
        compiler_params=pltpu.CompilerParams(vmem_limit_bytes=40 * MIB),
        name="project",
    )(plan, x, q, og, w, cos, sin)


def remote(src, dst, send, recv, device):
    return pltpu.make_async_remote_copy(
        src_ref=src, dst_ref=dst, send_sem=send, recv_sem=recv, device_id=device, device_id_type=MESH
    )


def greet(devices):
    barrier = pltpu.get_barrier_semaphore()
    for device in devices:
        pl.semaphore_signal(barrier, inc=1, device_id=device, device_id_type=MESH)
    pl.semaphore_wait(barrier, len(devices))


def spread_kernel(kv_s, q_s, g_s, h_s, kv_all, q_rx, g_rx, h_rx, kv1, q1, ss, rs, ys, yr, zs, zr):
    d, c = lax.axis_index("dp"), lax.axis_index("ctx")
    z, y = c // 4, c % 4
    dp_of = [(d + k) % 16 for k in range(16)]
    y_of = [(y + k) % 4 for k in range(4)]
    on_dp = lambda k: {"dp": dp_of[k]}
    on_y = lambda k: {"ctx": z * 4 + y_of[k]}
    up, down = {"ctx": (c + 4) % 16}, {"ctx": (c + 12) % 16}
    z_up, z_down = (z + 1) % 4, (z + 3) % 4

    greet([on_dp(k) for k in range(1, 16)] + [on_y(k) for k in range(1, 4)] + [up, down])

    kv_first = [remote(kv_s.at[dp_of[k]], kv1.at[d], ss.at[0, k], rs.at[0, k], on_dp(k)) for k in range(1, 16)]
    for copy in kv_first:
        copy.start()
    grads = [remote(g_s.at[y_of[k]], g_rx.at[y], ys.at[0, k], yr.at[0, k], on_y(k)) for k in range(1, 4)]
    for copy in grads:
        copy.start()
    q_first = [remote(q_s.at[dp_of[k]], q1.at[d], ss.at[1, k], rs.at[1, k], on_dp(k)) for k in range(1, 16)]
    for copy in q_first:
        copy.start()
    kv1[d] = kv_s[d]
    q1[d] = q_s[d]
    g_rx[y] = g_s[y]
    h_rx[y] = h_s[y]

    for copy in kv_first:
        copy.wait_recv()
    group = lambda k: pl.ds(pl.multiple_of(y_of[k] * 16, 16), 16)
    kv_second = [
        remote(kv1.at[:, group(k), :], kv_all.at[z, y], ys.at[1, k], yr.at[1, k], on_y(k)) for k in range(1, 4)
    ]
    for copy in kv_second:
        copy.start()
    kv_all[z, y] = kv1[:, group(0), :]

    chunk = [(y + 4 - t) % 4 for t in range(4)]
    own_up, own_down = [], []
    for t in range(4):
        if t:
            kv_second[t - 1].wait_recv()
        place = kv_all.at[z, chunk[t]]
        own_up.append(remote(place, place, zs.at[0, t], zr.at[0, t], up))
        own_down.append(remote(place, place, zs.at[1, t], zr.at[1, t], down))
        own_up[t].start()
        own_down[t].start()

    for copy in q_first:
        copy.wait_recv()
    heads = lambda k: pl.ds(pl.multiple_of(y_of[k] * 32, 32), 32)
    q_second = [remote(q1.at[:, heads(k), :], q_rx.at[y], ys.at[2, k], yr.at[2, k], on_y(k)) for k in range(1, 4)]
    for copy in q_second:
        copy.start()
    q_rx[y] = q1[:, heads(0), :]
    hidden = [remote(h_s.at[y_of[k]], h_rx.at[y], ys.at[3, k], yr.at[3, k], on_y(k)) for k in range(1, 4)]
    for copy in hidden:
        copy.start()

    passed = []
    for t in range(4):
        own_up[t].wait_recv()
        own_down[t].wait_recv()
        if t % 2 == 0:
            place = kv_all.at[z_down, chunk[t]]
            passed.append(remote(place, place, zs.at[2, t], zr.at[2, t], up))
        else:
            place = kv_all.at[z_up, chunk[t]]
            passed.append(remote(place, place, zs.at[2, t], zr.at[2, t], down))
        passed[t].start()
    for copy in passed + q_second + grads + hidden:
        copy.wait_recv()
    for copy in kv_first + grads + q_first + kv_second + own_up + own_down + q_second + hidden + passed:
        copy.wait_send()


def spread(kv, qs, gs, hs):
    return pl.pallas_call(
        spread_kernel,
        in_specs=[vm()] * 4,
        out_specs=[vm()] * 4,
        out_shape=[
            jax.ShapeDtypeStruct((4, 4, 16, 16, HD), BF),
            jax.ShapeDtypeStruct((4, 16, 32, HD), BF),
            jax.ShapeDtypeStruct((4, 16, 32, HD), BF),
            jax.ShapeDtypeStruct((4, 128, 1024), BF),
        ],
        scratch_shapes=[
            pltpu.VMEM((16, 64, HD), BF),
            pltpu.VMEM((16, 128, HD), BF),
            pltpu.SemaphoreType.DMA((2, 16)),
            pltpu.SemaphoreType.DMA((2, 16)),
            pltpu.SemaphoreType.DMA((4, 4)),
            pltpu.SemaphoreType.DMA((4, 4)),
            pltpu.SemaphoreType.DMA((3, 4)),
            pltpu.SemaphoreType.DMA((3, 4)),
        ],
        compiler_params=pltpu.CompilerParams(collective_id=0, has_side_effects=True, vmem_limit_bytes=40 * MIB),
        name="spread",
    )(kv, qs, gs, hs)


def attend_kernel(info, q, og, kv, first, att, qg, dkv, keys, vals, dk, dv, sc, big, low, out):
    step = pl.program_id(0)
    base = info[0]

    @pl.when(step == 0)
    def _():
        for i in range(4):
            block = kv[pl.ds(i * 64, 64)].astype(F32)
            keys[i * 512 : (i + 1) * 512, :] = block[:, :8, :].reshape(512, HD).astype(BF)
            vals[i * 512 : (i + 1) * 512, :] = block[:, 8:, :].reshape(512, HD).astype(BF)
        dk[...] = jnp.zeros_like(dk)
        dv[...] = jnp.zeros_like(dv)

    start = info[1 + step] // KB
    stop = (base + (step + 1) * 128 + KB - 1) // KB
    row = lax.broadcasted_iota(jnp.int32, (512, 1), 0)
    position = base + step * 128 + (row // 32) * 8 + row % 8
    lowest = first[...]

    big[...] = jnp.full_like(big, MASK_VALUE)

    def scores(kb, carry):
        cols = pl.ds(pl.multiple_of(kb * KB, KB), KB)
        s = rows_dot(q[...], keys[cols, :]) * SCALE
        index = kb * KB + lax.broadcasted_iota(jnp.int32, (512, KB), 1)
        s = jnp.where((index <= position) & (index >= lowest), s, MASK_VALUE)
        sc[:, cols] = s
        big[...] = jnp.maximum(big[...], jnp.maximum(s[:, :128], s[:, 128:]))
        return carry

    lax.fori_loop(start, stop, scores, 0)
    top = jnp.max(big[...], axis=1, keepdims=True)
    low[...] = jnp.zeros_like(low)

    def expo(kb, carry):
        cols = pl.ds(pl.multiple_of(kb * KB, KB), KB)
        e = jnp.exp(sc[:, cols] - top)
        sc[:, cols] = e
        low[...] += e[:, :128] + e[:, 128:]
        return carry

    lax.fori_loop(start, stop, expo, 0)
    inverse = 1.0 / jnp.sum(low[...], axis=1, keepdims=True)
    out[...] = jnp.zeros_like(out)

    def forward(kb, carry):
        cols = pl.ds(pl.multiple_of(kb * KB, KB), KB)
        p = sc[:, cols] * inverse
        sc[:, cols] = p
        rounded = p.astype(BF)
        out[...] += jnp.dot(rounded, vals[cols, :], preferred_element_type=F32)
        dv[cols, :] += cols_dot(rounded, og[...])
        return carry

    lax.fori_loop(start, stop, forward, 0)
    att[...] = out[...].astype(BF)
    delta = jnp.sum(out[...] * og[...].astype(F32), axis=1, keepdims=True)
    out[...] = jnp.zeros_like(out)

    def backward(kb, carry):
        cols = pl.ds(pl.multiple_of(kb * KB, KB), KB)
        dp = rows_dot(og[...], vals[cols, :])
        ds = (sc[:, cols] * (dp - delta)).astype(BF)
        out[...] += jnp.dot(ds, keys[cols, :], preferred_element_type=F32)
        dk[cols, :] += cols_dot(ds, q[...])
        return carry

    lax.fori_loop(start, stop, backward, 0)
    qg[...] = (out[...] * SCALE).astype(BF)

    @pl.when(step == 3)
    def _():
        for i in range(4):
            dkv[i, 0] = (dk[i * 512 : (i + 1) * 512, :] * SCALE).astype(BF)
            dkv[i, 1] = dv[i * 512 : (i + 1) * 512, :].astype(BF)


def attend(info, q, og, kv, first):
    full = lambda *shape: pl.BlockSpec(shape, lambda i, s: (0,) * len(shape))
    rows = lambda n: pl.BlockSpec((512, n), lambda i, s: (i, 0))
    return pl.pallas_call(
        attend_kernel,
        grid_spec=pltpu.PrefetchScalarGridSpec(
            num_scalar_prefetch=1,
            grid=(4,),
            in_specs=[rows(HD), rows(HD), full(256, 16, HD), rows(1)],
            out_specs=[rows(HD), rows(HD), full(4, 2, 512, HD)],
            scratch_shapes=[
                pltpu.VMEM((2048, HD), BF),
                pltpu.VMEM((2048, HD), BF),
                pltpu.VMEM((2048, HD), F32),
                pltpu.VMEM((2048, HD), F32),
                pltpu.VMEM((512, 2048), F32),
                pltpu.VMEM((512, HD), F32),
                pltpu.VMEM((512, HD), F32),
                pltpu.VMEM((512, HD), F32),
            ],
        ),
        out_shape=[
            jax.ShapeDtypeStruct((2048, HD), BF),
            jax.ShapeDtypeStruct((2048, HD), BF),
            jax.ShapeDtypeStruct((4, 2, 512, HD), BF),
        ],
        compiler_params=pltpu.CompilerParams(vmem_limit_bytes=48 * MIB),
        name="attend",
    )(info, q, og, kv, first)


def collect_kernel(att, qg, dkv, cos, sin, att_rx, qg_rx, pg_rx, src, own, hop, mid, fin, ys, yr, zs, zr, ss, rs):
    d, c = lax.axis_index("dp"), lax.axis_index("ctx")
    z, y = c // 4, c % 4
    dp_of = [(d + k) % 16 for k in range(16)]
    y_of = [(y + k) % 4 for k in range(4)]
    on_dp = lambda k: {"dp": dp_of[k]}
    on_y = lambda k: {"ctx": z * 4 + y_of[k]}
    up, down = {"ctx": (c + 4) % 16}, {"ctx": (c + 12) % 16}
    z_up, z_down, z_far = (z + 1) % 4, (z + 3) % 4, (z + 2) % 4

    greet([on_dp(k) for k in range(1, 16)] + [on_y(k) for k in range(1, 4)] + [up, down])

    far = [
        remote(dkv.at[z_far, 0], hop.at[0], zs.at[0], zr.at[0], down),
        remote(dkv.at[z_far, 1], hop.at[1], zs.at[1], zr.at[1], up),
    ]
    near = [
        remote(dkv.at[z_down, 1], fin.at[1, 0], zs.at[2], zr.at[2], down),
        remote(dkv.at[z_up, 0], fin.at[0, 0], zs.at[3], zr.at[3], up),
    ]
    for copy in far + near:
        copy.start()
    back = []
    for i, (a, b) in enumerate(((att, att_rx), (qg, qg_rx))):
        for k in range(1, 4):
            back.append(remote(a.at[y_of[k]], b.at[y], ys.at[i, k], yr.at[i, k], on_y(k)))
            back[-1].start()
        b[y] = a[y]

    far[0].wait_recv()
    mid[0] = (hop[0].astype(F32) + dkv[z_down, 0].astype(F32)).astype(BF)
    sums = [remote(mid.at[0], fin.at[0, 1], zs.at[4], zr.at[4], down)]
    sums[0].start()
    far[1].wait_recv()
    mid[1] = (hop[1].astype(F32) + dkv[z_up, 1].astype(F32)).astype(BF)
    sums.append(remote(mid.at[1], fin.at[1, 1], zs.at[5], zr.at[5], up))
    sums[1].start()
    for copy in near + sums:
        copy.wait_recv()
    for i in range(4):
        sl = slice(i * 128, (i + 1) * 128)
        total = lambda j: (
            dkv[z, j, sl, :].astype(F32) + fin[j, 0, sl, :].astype(F32) + fin[j, 1, sl, :].astype(F32)
        ).astype(BF).astype(F32)
        k = total(0)
        k = k * cos[sl, :] - pltpu.roll(k, 64, 1) * sin[sl, :]
        own[i] = jnp.concatenate([k.reshape(16, 8, HD), total(1).reshape(16, 8, HD)], 1).astype(BF)

    first = [remote(own.at[:, dp_of[k]], src.at[y, d], ss.at[k], rs.at[k], on_dp(k)) for k in range(1, 16)]
    for copy in first:
        copy.start()
    packed = [remote(own.at[y_of[k]], pg_rx.at[y], ys.at[2, k], yr.at[2, k], on_y(k)) for k in range(1, 4)]
    for copy in packed:
        copy.start()
    pg_rx[y] = own[y]
    src[y, d] = own[:, d]
    for copy in first:
        copy.wait_recv()
    gather = [remote(src.at[y], src.at[y], ys.at[3, k], yr.at[3, k], on_y(k)) for k in range(1, 4)]
    for copy in gather:
        copy.start()
    for copy in back + packed + gather:
        copy.wait_recv()
    for copy in far + near + back + sums + first + packed + gather:
        copy.wait_send()


def collect(att, qg, dkv, cos, sin):
    return pl.pallas_call(
        collect_kernel,
        in_specs=[vm()] * 5,
        out_specs=[vm()] * 4,
        out_shape=[
            jax.ShapeDtypeStruct((4, 512, HD), BF),
            jax.ShapeDtypeStruct((4, 512, HD), BF),
            jax.ShapeDtypeStruct((4, 16, 16, HD), BF),
            jax.ShapeDtypeStruct((4, 16, 4, 16, HD), BF),
        ],
        scratch_shapes=[
            pltpu.VMEM((4, 16, 16, HD), BF),
            pltpu.VMEM((2, 512, HD), BF),
            pltpu.VMEM((2, 512, HD), BF),
            pltpu.VMEM((2, 2, 512, HD), BF),
            pltpu.SemaphoreType.DMA((4, 4)),
            pltpu.SemaphoreType.DMA((4, 4)),
            pltpu.SemaphoreType.DMA((6,)),
            pltpu.SemaphoreType.DMA((6,)),
            pltpu.SemaphoreType.DMA((16,)),
            pltpu.SemaphoreType.DMA((16,)),
        ],
        compiler_params=pltpu.CompilerParams(collective_id=1, has_side_effects=True, vmem_limit_bytes=40 * MIB),
        name="collect",
    )(att, qg, dkv, cos, sin)


def weight_kernel(src, hs, tile, pgm):
    step = pl.program_id(0)

    @pl.when(step == 0)
    def _():
        for g in range(4):
            for i in range(4):
                block = src[g, :, i].astype(F32)
                pgm[i * 128 : (i + 1) * 128, g * HD : (g + 1) * HD] = block[:, :8, :].reshape(128, HD).astype(BF)
                pgm[i * 128 : (i + 1) * 128, (4 + g) * HD : (5 + g) * HD] = (
                    block[:, 8:, :].reshape(128, HD).astype(BF)
                )

    t = cols_dot(pgm[...], hs[...])
    tile[...] = t.reshape(16, 1, 64, 256).astype(BF)


def weight(src, hs):
    return pl.pallas_call(
        weight_kernel,
        grid=(4,),
        in_specs=[
            pl.BlockSpec((4, 16, 4, 16, HD), lambda i: (0, 0, 0, 0, 0)),
            pl.BlockSpec((512, 256), lambda i: (0, i)),
        ],
        out_specs=pl.BlockSpec((16, 1, 64, 256), lambda i: (0, i, 0, 0)),
        out_shape=jax.ShapeDtypeStruct((16, 4, 64, 256), BF),
        scratch_shapes=[pltpu.VMEM((512, 1024), BF)],
        compiler_params=pltpu.CompilerParams(vmem_limit_bytes=40 * MIB),
        name="weight",
    )(src, hs)


def reduce_kernel(tile, grad, pair, mine, ring, part, last, cs, cr, xs, xr, zs, zr):
    d, c = lax.axis_index("dp"), lax.axis_index("ctx")
    zl, x, core = d // 8, (d // 2) % 4, d % 2
    z, y = c // 4, c % 4
    x_of = [(x + k) % 4 for k in range(4)]
    sibling = {"dp": d + 1 - 2 * core}
    on_x = lambda k: {"dp": zl * 8 + x_of[k] * 2 + core}
    zz = zl * 4 + z
    z_of = [(zz + k) % 8 for k in range(8)]
    on_z = lambda k: {"dp": (z_of[k] // 4) * 8 + x * 2 + core, "ctx": (z_of[k] % 4) * 4 + y}

    greet([sibling] + [on_x(k) for k in range(1, 4)] + [on_z(k) for k in range(1, 8)])

    order = [2, 1, 3, 0]
    swaps = [
        remote(tile.at[:, x_of[k], 1 - core], pair.at[:, x_of[k]], cs.at[k], cr.at[k], sibling) for k in order
    ]
    for copy in swaps:
        copy.start()
    sums = []
    for copy, k in zip(swaps, order):
        copy.wait_recv()
        for a in range(2):
            for b in range(4):
                mine[k, a, b] = (
                    tile[a, x_of[k], core, b].astype(F32) + pair[a, x_of[k], b].astype(F32)
                ).astype(BF)
        if k:
            sums.append(remote(mine.at[k], ring.at[k], xs.at[k], xr.at[k], on_x(k)))
            sums[-1].start()
    for copy in sums:
        copy.wait_recv()
    for a in range(2):
        for b in range(4):
            t = mine[0, a, b].astype(F32)
            for k in range(1, 4):
                t = t + ring[k, a, b].astype(F32)
            part[a * 4 + b] = t.astype(BF)
    ends = [remote(part.at[z_of[k]], last.at[k], zs.at[k], zr.at[k], on_z(k)) for k in range(1, 8)]
    for copy in ends:
        copy.start()
    for copy in ends:
        copy.wait_recv()
    t = part[zz].astype(F32)
    for k in range(1, 8):
        t = t + last[k].astype(F32)
    grad[...] = t * (1.0 / 16.0)
    for copy in swaps + sums + ends:
        copy.wait_send()


def reduce_tiles(tile):
    return pl.pallas_call(
        reduce_kernel,
        in_specs=[vm()],
        out_specs=vm(),
        out_shape=jax.ShapeDtypeStruct((64, 256), F32),
        scratch_shapes=[
            pltpu.VMEM((2, 4, 4, 64, 256), BF),
            pltpu.VMEM((4, 2, 4, 64, 256), BF),
            pltpu.VMEM((4, 2, 4, 64, 256), BF),
            pltpu.VMEM((8, 64, 256), BF),
            pltpu.VMEM((8, 64, 256), BF),
            pltpu.SemaphoreType.DMA((4,)),
            pltpu.SemaphoreType.DMA((4,)),
            pltpu.SemaphoreType.DMA((4,)),
            pltpu.SemaphoreType.DMA((4,)),
            pltpu.SemaphoreType.DMA((8,)),
            pltpu.SemaphoreType.DMA((8,)),
        ],
        compiler_params=pltpu.CompilerParams(collective_id=2, has_side_effects=True, vmem_limit_bytes=40 * MIB),
        name="reduce_tiles",
    )(tile)


def finish_kernel(att, qg, pg, w1, w2, att_o, qg_o, hg_o, pgm):
    step = pl.program_id(0)

    @pl.when(step == 0)
    def _():
        for g in range(4):
            block = pg[g].astype(F32)
            pgm[:, g * HD : (g + 1) * HD] = block[:, :8, :].reshape(128, HD).astype(BF)
            pgm[:, (4 + g) * HD : (5 + g) * HD] = block[:, 8:, :].reshape(128, HD).astype(BF)
            for source, target in ((att, att_o), (qg, qg_o)):
                block = source[g].reshape(16, 32, HD).astype(F32)
                for h in range(4):
                    cols = slice((g * 4 + h) * HD, (g * 4 + h + 1) * HD)
                    target[:, cols] = block[:, h * 8 : h * 8 + 8, :].reshape(128, HD).astype(BF)

    hg_o[...] = (
        jnp.dot(pgm[:, :512], w1[...], preferred_element_type=F32)
        + jnp.dot(pgm[:, 512:], w2[...], preferred_element_type=F32)
    ).astype(BF)


def finish(att, qg, pg, w):
    full = lambda *shape: pl.BlockSpec(shape, lambda i: (0,) * len(shape))
    return pl.pallas_call(
        finish_kernel,
        grid=(8,),
        in_specs=[
            full(4, 512, HD), full(4, 512, HD), full(4, 16, 16, HD),
            pl.BlockSpec((512, 512), lambda i: (0, i)), pl.BlockSpec((512, 512), lambda i: (1, i)),
        ],
        out_specs=[full(128, 2048), full(128, 2048), pl.BlockSpec((128, 512), lambda i: (0, i))],
        out_shape=[
            jax.ShapeDtypeStruct((128, 2048), BF),
            jax.ShapeDtypeStruct((128, 2048), BF),
            jax.ShapeDtypeStruct((128, 4096), BF),
        ],
        scratch_shapes=[pltpu.VMEM((128, 1024), BF)],
        compiler_params=pltpu.CompilerParams(vmem_limit_bytes=40 * MIB),
        name="finish",
    )(att, qg, pg, w, w)


def body(hidden_rows, query_rows, out_grad, projection, packing_plan, document_ids):
    d, c = lax.axis_index("dp"), lax.axis_index("ctx")
    z = c // 4
    near_cos, near_sin = angle_tables(c * 128 + d * 8 + jnp.arange(8, dtype=jnp.int32))
    cos, sin = angle_tables(z * 512 + jnp.arange(512, dtype=jnp.int32))
    documents = document_ids[0]
    own_documents = lax.dynamic_slice_in_dim(documents, z * 512, 512)
    first = jnp.sum((documents[None, :] < own_documents[:, None]).astype(jnp.int32), axis=1)
    info = jnp.concatenate([(z * 512)[None].astype(jnp.int32), first[::128]])
    first_rows = jnp.broadcast_to(first.reshape(64, 1, 8), (64, 4, 8)).reshape(2048, 1)

    kv, qs, gs, hs = project(packing_plan, hidden_rows, query_rows, out_grad, projection, near_cos, near_sin)
    kv_all, q_rx, g_rx, h_rx = spread(kv, qs, gs, hs)
    att, qg, dkv = attend(
        info, q_rx.reshape(2048, HD), g_rx.reshape(2048, HD), kv_all.reshape(256, 16, HD), first_rows
    )
    att_rx, qg_rx, pg_rx, src = collect(att.reshape(4, 512, HD), qg.reshape(4, 512, HD), dkv, cos, sin)
    tile = weight(src, h_rx.reshape(512, 1024))
    attended, query_grad, hidden_grad = finish(att_rx, qg_rx, pg_rx, projection)
    weight_grad = reduce_tiles(tile.reshape(2, 4, 2, 4, 64, 256))
    return attended, query_grad, hidden_grad, weight_grad


def solution(mesh):
    rows = P(("dp", "ctx"), None)
    return jax.shard_map(
        body,
        mesh=mesh,
        in_specs=(rows, rows, rows, P(), rows, P("dp", None)),
        out_specs=(rows, rows, rows, P("dp", "ctx")),
        check_vma=False,
    )
```

time: 541 us -> 180 us (0.33)
  waiting for transfers between devices: 317 us -> 0 us
  Pallas kernels: 0 us -> 162 us
  matrix products: 74.6 us -> 0 us
  starting transfers between devices: 47.2 us -> 0 us
  blocking collectives: 27.5 us -> 0 us
  other arithmetic: 22.5 us -> 2.07 us
  between operations: 14.1 us -> 0.77 us
  local copies, waits for them, and re-layouts: 25.9 us -> 15.6 us
  loops' own time: 8.02 us -> 0 us
    reduce_scatter x2 -> x0, waiting for transfers between devices: 168 us -> none  [the longest x1 131 us: body(): lax.psum_scatter(block_term.astype(jnp.bfloat16), 'ctx', scatter_dimensio...]
    pallas_call x0 -> x7, Pallas kernels: none -> 162 us  [the longest x1 67.6 us: collect(): pl.pallas_call(collect_kernel, in_specs=[vm()] * 5, out_specs=[vm()] * 4,...]
    all_gather x2 -> x0, waiting for transfers between devices: 84.4 us -> none  [the longest x1 56.8 us: body(): lax.all_gather(values.reshape(row_count, key_width), 'ctx', axis=0, tiled...]
    dot_general x27 -> x0, matrix products: 74.6 us -> none  [the longest x9 32.8 us: outer_rows(): lax.dot_general(left_side, right_side, (((0,), (0,)), ((), ())), preferre...]
    all_to_all x7 -> x0, waiting for transfers between devices: 64 us -> none  [the longest x1 15.4 us: body(): lax.all_to_all(send_hidden, 'dp', split_axis=0, concat_axis=0, tiled=True)]
    all_to_all x7 -> x0, starting transfers between devices: 47 us -> none  [the longest x1 10.5 us: body(): lax.all_to_all(out_grad, 'ctx', split_axis=1, concat_axis=0, tiled=True)]
    all_to_all x1 -> x0, blocking collectives: 27.5 us -> none  [body(): lax.all_to_all(key_total, 'ctx', split_axis=0, concat_axis=1, tiled=True)]
    unnamed x12 -> x23, local copies, waits for them, and re-layouts: 4.24 us -> 15 us
  transfers between devices with their start and end apart: 11 -> 0, of which waited for: 9 -> 0; matrix products, arithmetic and copies ran while one was open for 4% -> 0% of each run, Pallas kernels for 0% -> 0%
where the time goes in v1:
time: 180 us
  Pallas kernels  162 us (90%)
  local copies, waits for them, and re-layouts  15.6 us (9%)
  other arithmetic  2.07 us (1%)
    pallas_call x1, Pallas kernels, collect(): pl.pallas_call(collect_kernel, in_specs=[vm()] * 5, out_specs=[vm()] * 4,...  67.6 us
    pallas_call x1, Pallas kernels, spread(): pl.pallas_call(spread_kernel, in_specs=[vm()] * 4, out_specs=[vm()] * 4,...  45 us
    pallas_call x1, Pallas kernels, reduce_tiles(): pl.pallas_call(reduce_kernel, in_specs=[vm()], out_specs=vm(), out_shape=...  27.8 us
    unnamed x23, local copies, waits for them, and re-layouts  15 us
    pallas_call x1, Pallas kernels, attend(): pl.pallas_call(attend_kernel, grid_spec=pltpu.PrefetchScalarGridSpec(num_...  9.68 us
    pallas_call x1, Pallas kernels, finish(): pl.pallas_call(finish_kernel, grid=(8,), in_specs=[full(4, 512, HD), full...  5.04 us
    pallas_call x1, Pallas kernels, project(): pl.pallas_call(project_kernel, grid=(4,), in_specs=[full(1, 128), full(12...  4.06 us

profile of v1, /device:TPU:1, one launch (start us, length us, event | category | flops | bytes accessed | tf_op | source)
XLA Modules:
  0.0 180.0 jit_solution(3777381497302598260)
XLA Ops:
  0.7 0.1 fusion.1
  0.8 0.1 pad_maximum_fusion.2
  0.9 0.0 copy-start
  0.9 3.4 %copy-done = bf16[1024,4096]{1,0:T(8,128)(2,1)S(1)} copy-done((bf16[1024,4096]{1,0:T(8,128)(2,1)S(1)}, bf16[1024,4096]{1,0:T(8,128)(2,1)}, u32[]{:S(2)}) %copy-start) | copy-done | bytes 8388632
  4.2 0.0 copy-start.2
  4.2 1.2 copy-done.2
  5.5 1.0 copy-done.3
  6.5 1.0 copy-done.4
  7.6 0.7 copy-done.9
  8.2 4.1 %project.1 = (bf16[16,64,128]{2,1,0:T(8,128)(2,1)S(1)}, bf16[16,128,128]{2,1,0:T(8,128)(2,1)S(1)}, bf16[4,16,32,128]{3,2,1,0:T(8,128)(2,1)S(1)}, bf16[4,128,1024]{2,1,0:T(8,128)(2,1)S(1)}) custom-call(s32[1,128]{1,0:T(1,128)S(1)} %copy-done.9, bf16[128,4096]{1,0:T(8,128)(2,1)S(1)} %copy-done.2, bf16[128,2048]{1,0:T(8,128)(2,1)S(1)} %copy-done.3, ...), custom_call_target="tpu_custom_call" | custom-call | tf_op jit(solution)/shard_map/project/pallas_call | solution.py:78
  12.3 45.0 %spread.1 = (bf16[4,4,16,16,128]{4,3,2,1,0:T(8,128)(2,1)S(1)}, bf16[4,16,32,128]{3,2,1,0:T(8,128)(2,1)S(1)}, bf16[4,16,32,128]{3,2,1,0:T(8,128)(2,1)S(1)}, bf16[4,128,1024]{2,1,0:T(8,128)(2,1)S(1)}) custom-call(bf16[16,64,128]{2,1,0:T(8,128)(2,1)S(1)} %get-tuple-element.22.kv_s, bf16[16,128,128]{2,1,0:T(8,128)(2,1)S(1)} %get-tuple-element.23.q_s, ...), custom_call_target="tpu_custom_call" | custom-call | tf_op jit(solution)/shard_map/spread/pallas_call | solution.py:187
  57.3 0.0 copy-start.5
  57.3 0.8 copy-done.5
  58.1 0.8 copy-done.7
  58.9 0.0 copy-done.10
  58.9 0.6 convert_reduce_fusion
  59.5 0.1 broadcast_in_dim.7
  59.6 0.3 reshape.60.first
  60.0 0.1 slice.3
  60.0 0.1 pad_add_fusion.info
  60.1 1.0 copy-done.6
  61.2 1.0 copy-done.8
  62.2 9.7 %attend.1 = (bf16[2048,128]{1,0:T(8,128)(2,1)S(1)}, bf16[2048,128]{1,0:T(8,128)(2,1)S(1)}, bf16[4,2,512,128]{3,2,1,0:T(8,128)(2,1)S(1)}) custom-call(s32[5]{0:T(128)S(1)} %pad_add_fusion.info, bf16[2048,128]{1,0:T(8,128)(2,1)S(1)} %bitcast.15, bf16[2048,128]{1,0:T(8,128)(2,1)S(1)} %bitcast.16, bf16[256,16,128]{2,1,0:T(8,128)(2,1)S(1)} %bitcast.11, ...), custom_call_target="tpu_custom_call" | custom-call | tf_op jit(solution)/shard_map/attend/pallas_call | solution.py:292
  71.9 1.0 fusion
  72.9 0.2 pad_maximum_fusion
  73.1 67.6 %collect.1 = (bf16[4,512,128]{2,1,0:T(8,128)(2,1)S(1)}, bf16[4,512,128]{2,1,0:T(8,128)(2,1)S(1)}, bf16[4,16,16,128]{3,2,1,0:T(8,128)(2,1)S(1)}, bf16[4,16,4,16,128]{4,3,2,1,0:T(8,128)(2,1)S(1)}) custom-call(bf16[4,512,128]{2,1,0:T(8,128)(2,1)S(1)} %bitcast.13, bf16[4,512,128]{2,1,0:T(8,128)(2,1)S(1)} %bitcast.14, ...), custom_call_target="tpu_custom_call" | custom-call | tf_op jit(solution)/shard_map/collect/pallas_call | solution.py:388
  140.7 2.5 %weight.1 = bf16[16,4,64,256]{3,2,1,0:T(8,128)(2,1)S(1)} custom-call(bf16[4,16,4,16,128]{4,3,2,1,0:T(8,128)(2,1)S(1)} %get-tuple-element.38.src, bf16[512,1024]{1,0:T(8,128)(2,1)S(1)} %bitcast.12), custom_call_target="tpu_custom_call" | custom-call | tf_op jit(solution)/shard_map/weight/pallas_call | solution.py:433
  143.2 27.8 %reduce_tiles.1 = f32[64,256]{1,0:T(8,128)S(1)} custom-call(bf16[2,4,2,4,64,256]{5,4,3,2,1,0:T(8,128)(2,1)S(1)} %bitcast.10), custom_call_target="tpu_custom_call" | custom-call | tf_op jit(solution)/shard_map/reduce_tiles/pallas_call | solution.py:500
  171.0 0.0 copy-start.1
  171.0 3.4 %copy-done.1 = bf16[1024,4096]{1,0:T(8,128)(2,1)S(1)} copy-done((bf16[1024,4096]{1,0:T(8,128)(2,1)S(1)}, bf16[1024,4096]{1,0:T(8,128)(2,1)}, u32[]{:S(2)}) %copy-start.1) | copy-done | bytes 8388632
  174.3 5.0 %finish.1 = (bf16[128,2048]{1,0:T(8,128)(2,1)}, bf16[128,2048]{1,0:T(8,128)(2,1)}, bf16[128,4096]{1,0:T(8,128)(2,1)}) custom-call(bf16[4,512,128]{2,1,0:T(8,128)(2,1)S(1)} %get-tuple-element.32.att, bf16[4,512,128]{2,1,0:T(8,128)(2,1)S(1)} %get-tuple-element.33.qg, bf16[4,16,16,128]{3,2,1,0:T(8,128)(2,1)S(1)} %get-tuple-element.34.pg, ...), custom_call_target="tpu_custom_call" | custom-call | tf_op jit(solution)/shard_map/finish/pallas_call | solution.py:546
  179.4 0.6 copy.13
  (12 shorter events, 0.1 us)
Async XLA Ops:
  0.9 3.4 %copy-start = (bf16[1024,4096]{1,0:T(8,128)(2,1)S(1)}, bf16[1024,4096]{1,0:T(8,128)(2,1)}, u32[]{:S(2)}) copy-start(bf16[1024,4096]{1,0:T(8,128)(2,1)} %w2.1) | copy-start | bytes 25165828
  4.2 1.2 copy-start.2
  5.5 1.0 copy-start.3
  6.5 1.0 copy-start.4
  7.6 0.7 copy-start.9
  8.2 50.7 %copy-start.10 = (s32[1,2048]{1,0:T(1,128)S(1)}, s32[1,2048]{1,0:T(1,128)}, u32[]{:S(2)}) copy-start(s32[1,2048]{1,0:T(1,128)} %param.11) | copy-start | bytes 24580
  57.3 0.8 copy-start.5
  58.1 0.8 copy-start.7
  60.1 1.0 copy-start.6
  61.2 1.0 copy-start.8
  171.0 3.4 %copy-start.1 = (bf16[1024,4096]{1,0:T(8,128)(2,1)S(1)}, bf16[1024,4096]{1,0:T(8,128)(2,1)}, u32[]{:S(2)}) copy-start(bf16[1024,4096]{1,0:T(8,128)(2,1)} %w2.1) | copy-start | bytes 25165828

commit v2 on v1

--- a/solution.py
+++ b/solution.py
@@ -209,104 +209,108 @@
     )(kv, qs, gs, hs)
 
 
-def attend_kernel(info, q, og, kv, first, att, qg, dkv, keys, vals, dk, dv, sc, big, low, out):
-    step = pl.program_id(0)
+def attend_kernel(info, q, og, kv, first, att, qg, dkv, keys, vals, keys_t, vals_t, dk, dv, sc, gp, q_t, og_t, out_t, grad_t):
     base = info[0]
-
-    @pl.when(step == 0)
-    def _():
-        for i in range(4):
-            block = kv[pl.ds(i * 64, 64)].astype(F32)
-            keys[i * 512 : (i + 1) * 512, :] = block[:, :8, :].reshape(512, HD).astype(BF)
-            vals[i * 512 : (i + 1) * 512, :] = block[:, 8:, :].reshape(512, HD).astype(BF)
-        dk[...] = jnp.zeros_like(dk)
-        dv[...] = jnp.zeros_like(dv)
-
-    start = info[1 + step] // KB
-    stop = (base + (step + 1) * 128 + KB - 1) // KB
-    row = lax.broadcasted_iota(jnp.int32, (512, 1), 0)
-    position = base + step * 128 + (row // 32) * 8 + row % 8
-    lowest = first[...]
-
-    big[...] = jnp.full_like(big, MASK_VALUE)
-
-    def scores(kb, carry):
-        cols = pl.ds(pl.multiple_of(kb * KB, KB), KB)
-        s = rows_dot(q[...], keys[cols, :]) * SCALE
-        index = kb * KB + lax.broadcasted_iota(jnp.int32, (512, KB), 1)
-        s = jnp.where((index <= position) & (index >= lowest), s, MASK_VALUE)
-        sc[:, cols] = s
-        big[...] = jnp.maximum(big[...], jnp.maximum(s[:, :128], s[:, 128:]))
+    for i in range(4):
+        block = kv[pl.ds(i * 64, 64)].astype(F32)
+        rows = slice(i * 512, (i + 1) * 512)
+        k = block[:, :8, :].reshape(512, HD)
+        v = block[:, 8:, :].reshape(512, HD)
+        keys[rows, :] = k.astype(BF)
+        vals[rows, :] = v.astype(BF)
+        keys_t[:, rows] = k.T.astype(BF)
+        vals_t[:, rows] = v.T.astype(BF)
+    keys[2048:, :] = jnp.zeros((128, HD), BF)
+    vals[2048:, :] = jnp.zeros((128, HD), BF)
+    keys_t[:, 2048:] = jnp.zeros((HD, 128), BF)
+    vals_t[:, 2048:] = jnp.zeros((HD, 128), BF)
+    dk[...] = jnp.zeros_like(dk)
+    dv[...] = jnp.zeros_like(dv)
+    fold = SCALE * math.log2(math.e)
+
+    def query_block(qb, carry):
+        here = pl.ds(pl.multiple_of(qb * 512, 512), 512)
+        q_t[...] = q[here, :].astype(F32).T.astype(BF)
+        og_t[...] = og[here, :].astype(F32).T.astype(BF)
+        start = (info[1 + qb] // 128) * 128
+        count = (base + (qb + 1) * 128 - start + KB - 1) // KB
+        lane = lax.broadcasted_iota(jnp.int32, (1, 512), 1)
+        position = base + qb * 128 + (lane // 32) * 8 + lane % 8
+        lowest = first[qb]
+        out_t[...] = jnp.zeros_like(out_t)
+        grad_t[...] = jnp.zeros_like(grad_t)
+
+        def eights(t):
+            return t.reshape(KB // 8, 8, 512)
+
+        def scores(i, top):
+            at = pl.multiple_of(start + i * KB, 128)
+            rows = pl.ds(at, KB)
+            s = jnp.dot(keys[rows, :], q_t[...], preferred_element_type=F32)
+            index = at + lax.broadcasted_iota(jnp.int32, (KB, 512), 0)
+            s = jnp.where((index <= position) & (index >= lowest), s, MASK_VALUE)
+            sc[rows, :] = s
+            return jnp.maximum(top, jnp.max(eights(s), axis=0))
+
+        top = lax.fori_loop(0, count, scores, jnp.full((8, 512), MASK_VALUE, F32))
+        top = jnp.max(top, axis=0, keepdims=True) * fold
+
+        def expo(i, sums):
+            rows = pl.ds(pl.multiple_of(start + i * KB, 128), KB)
+            e = jnp.exp2(sc[rows, :] * fold - top)
+            grad = jnp.dot(vals[rows, :], og_t[...], preferred_element_type=F32)
+            sc[rows, :] = e
+            gp[rows, :] = grad
+            return sums[0] + jnp.sum(eights(e), axis=0), sums[1] + jnp.sum(eights(e * grad), axis=0)
+
+        zero = jnp.zeros((8, 512), F32)
+        total, product = lax.fori_loop(0, count, expo, (zero, zero))
+        inverse = 1.0 / jnp.sum(total, axis=0, keepdims=True)
+        delta = jnp.sum(product, axis=0, keepdims=True) * inverse
+
+        def both(i, c):
+            at = pl.multiple_of(start + i * KB, 128)
+            rows = pl.ds(at, KB)
+            p = sc[rows, :] * inverse
+            rounded = p.astype(BF)
+            ds = (p * (gp[rows, :] - delta)).astype(BF)
+            dv[rows, :] += jnp.dot(rounded, og[here, :], preferred_element_type=F32)
+            dk[rows, :] += jnp.dot(ds, q[here, :], preferred_element_type=F32)
+            out_t[...] += jnp.dot(vals_t[:, rows], rounded, preferred_element_type=F32)
+            grad_t[...] += jnp.dot(keys_t[:, rows], ds, preferred_element_type=F32)
+            return c
+
+        lax.fori_loop(0, count, both, 0)
+        att[here, :] = out_t[...].T.astype(BF)
+        qg[here, :] = (grad_t[...] * SCALE).T.astype(BF)
         return carry
 
-    lax.fori_loop(start, stop, scores, 0)
-    top = jnp.max(big[...], axis=1, keepdims=True)
-    low[...] = jnp.zeros_like(low)
-
-    def expo(kb, carry):
-        cols = pl.ds(pl.multiple_of(kb * KB, KB), KB)
-        e = jnp.exp(sc[:, cols] - top)
-        sc[:, cols] = e
-        low[...] += e[:, :128] + e[:, 128:]
-        return carry
-
-    lax.fori_loop(start, stop, expo, 0)
-    inverse = 1.0 / jnp.sum(low[...], axis=1, keepdims=True)
-    out[...] = jnp.zeros_like(out)
-
-    def forward(kb, carry):
-        cols = pl.ds(pl.multiple_of(kb * KB, KB), KB)
-        p = sc[:, cols] * inverse
-        sc[:, cols] = p
-        rounded = p.astype(BF)
-        out[...] += jnp.dot(rounded, vals[cols, :], preferred_element_type=F32)
-        dv[cols, :] += cols_dot(rounded, og[...])
-        return carry
-
-    lax.fori_loop(start, stop, forward, 0)
-    att[...] = out[...].astype(BF)
-    delta = jnp.sum(out[...] * og[...].astype(F32), axis=1, keepdims=True)
-    out[...] = jnp.zeros_like(out)
-
-    def backward(kb, carry):
-        cols = pl.ds(pl.multiple_of(kb * KB, KB), KB)
-        dp = rows_dot(og[...], vals[cols, :])
-        ds = (sc[:, cols] * (dp - delta)).astype(BF)
-        out[...] += jnp.dot(ds, keys[cols, :], preferred_element_type=F32)
-        dk[cols, :] += cols_dot(ds, q[...])
-        return carry
-
-    lax.fori_loop(start, stop, backward, 0)
-    qg[...] = (out[...] * SCALE).astype(BF)
-
-    @pl.when(step == 3)
-    def _():
-        for i in range(4):
-            dkv[i, 0] = (dk[i * 512 : (i + 1) * 512, :] * SCALE).astype(BF)
-            dkv[i, 1] = dv[i * 512 : (i + 1) * 512, :].astype(BF)
+    lax.fori_loop(0, 4, query_block, 0)
+    for i in range(4):
+        rows = slice(i * 512, (i + 1) * 512)
+        dkv[i, 0] = (dk[rows, :] * SCALE).astype(BF)
+        dkv[i, 1] = dv[rows, :].astype(BF)
 
 
 def attend(info, q, og, kv, first):
-    full = lambda *shape: pl.BlockSpec(shape, lambda i, s: (0,) * len(shape))
-    rows = lambda n: pl.BlockSpec((512, n), lambda i, s: (i, 0))
     return pl.pallas_call(
         attend_kernel,
-        grid_spec=pltpu.PrefetchScalarGridSpec(
-            num_scalar_prefetch=1,
-            grid=(4,),
-            in_specs=[rows(HD), rows(HD), full(256, 16, HD), rows(1)],
-            out_specs=[rows(HD), rows(HD), full(4, 2, 512, HD)],
-            scratch_shapes=[
-                pltpu.VMEM((2048, HD), BF),
-                pltpu.VMEM((2048, HD), BF),
-                pltpu.VMEM((2048, HD), F32),
-                pltpu.VMEM((2048, HD), F32),
-                pltpu.VMEM((512, 2048), F32),
-                pltpu.VMEM((512, HD), F32),
-                pltpu.VMEM((512, HD), F32),
-                pltpu.VMEM((512, HD), F32),
-            ],
-        ),
+        in_specs=[pl.BlockSpec(memory_space=pltpu.SMEM)] + [vm()] * 4,
+        out_specs=[vm()] * 3,
+        scratch_shapes=[
+            pltpu.VMEM((2176, HD), BF),
+            pltpu.VMEM((2176, HD), BF),
+            pltpu.VMEM((HD, 2176), BF),
+            pltpu.VMEM((HD, 2176), BF),
+            pltpu.VMEM((2176, HD), F32),
+            pltpu.VMEM((2176, HD), F32),
+            pltpu.VMEM((2176, 512), F32),
+            pltpu.VMEM((2176, 512), F32),
+            pltpu.VMEM((HD, 512), BF),
+            pltpu.VMEM((HD, 512), BF),
+            pltpu.VMEM((HD, 512), F32),
+            pltpu.VMEM((HD, 512), F32),
+        ],
         out_shape=[
             jax.ShapeDtypeStruct((2048, HD), BF),
             jax.ShapeDtypeStruct((2048, HD), BF),
@@ -571,7 +575,7 @@
     own_documents = lax.dynamic_slice_in_dim(documents, z * 512, 512)
     first = jnp.sum((documents[None, :] < own_documents[:, None]).astype(jnp.int32), axis=1)
     info = jnp.concatenate([(z * 512)[None].astype(jnp.int32), first[::128]])
-    first_rows = jnp.broadcast_to(first.reshape(64, 1, 8), (64, 4, 8)).reshape(2048, 1)
+    first_rows = jnp.broadcast_to(first.reshape(64, 1, 8), (64, 4, 8)).reshape(4, 1, 512)
 
     kv, qs, gs, hs = project(packing_plan, hidden_rows, query_rows, out_grad, projection, near_cos, near_sin)
     kv_all, q_rx, g_rx, h_rx = spread(kv, qs, gs, hs)

time: 180 us -> 160 us (0.89)
  Pallas kernels: 162 us -> 146 us
  local copies, waits for them, and re-layouts: 15.6 us -> 11.7 us
    pallas_call x1, Pallas kernels: 67.6 us -> 53.9 us  [collect(): pl.pallas_call(collect_kernel, in_specs=[vm()] * 5, out_specs=[vm()] * 4,...]
    unnamed x23 -> x15, local copies, waits for them, and re-layouts: 15 us -> 11.4 us
    pallas_call x1, Pallas kernels: 9.68 us -> 6.33 us  [attend(): pl.pallas_call(attend_kernel, in_specs=[pl.BlockSpec(memory_space=pltpu.S...]
where the time goes in v2:
time: 160 us
  Pallas kernels  146 us (91%)
  local copies, waits for them, and re-layouts  11.7 us (7%)
  other arithmetic  2.07 us (1%)
    pallas_call x1, Pallas kernels, collect(): pl.pallas_call(collect_kernel, in_specs=[vm()] * 5, out_specs=[vm()] * 4,...  53.9 us
    pallas_call x1, Pallas kernels, spread(): pl.pallas_call(spread_kernel, in_specs=[vm()] * 4, out_specs=[vm()] * 4,...  45 us
    pallas_call x1, Pallas kernels, reduce_tiles(): pl.pallas_call(reduce_kernel, in_specs=[vm()], out_specs=vm(), out_shape=...  28.8 us
    unnamed x15, local copies, waits for them, and re-layouts  11.4 us
    pallas_call x1, Pallas kernels, attend(): pl.pallas_call(attend_kernel, in_specs=[pl.BlockSpec(memory_space=pltpu.S...  6.33 us
    pallas_call x1, Pallas kernels, finish(): pl.pallas_call(finish_kernel, grid=(8,), in_specs=[full(4, 512, HD), full...  5.04 us
    pallas_call x1, Pallas kernels, project(): pl.pallas_call(project_kernel, grid=(4,), in_specs=[full(1, 128), full(12...  4.06 us

profile of v2, /device:TPU:1, one launch (start us, length us, event | category | flops | bytes accessed | tf_op | source)
XLA Modules:
  0.0 160.2 jit_solution(17679203726217442465)
XLA Ops:
  0.7 0.1 fusion.1
  0.8 0.1 pad_maximum_fusion.2
  0.9 0.0 copy-start
  0.9 3.4 %copy-done = bf16[1024,4096]{1,0:T(8,128)(2,1)S(1)} copy-done((bf16[1024,4096]{1,0:T(8,128)(2,1)S(1)}, bf16[1024,4096]{1,0:T(8,128)(2,1)}, u32[]{:S(2)}) %copy-start) | copy-done | bytes 8388632
  4.2 0.0 copy-start.2
  4.2 1.2 copy-done.2
  5.5 0.0 copy-start.3
  5.5 1.0 copy-done.3
  6.5 0.0 copy-start.4
  6.5 1.0 copy-done.4
  7.6 0.0 copy-start.5
  7.6 0.7 copy-done.5
  8.2 0.0 copy-start.6
  8.2 4.1 %project.1 = (bf16[16,64,128]{2,1,0:T(8,128)(2,1)S(1)}, bf16[16,128,128]{2,1,0:T(8,128)(2,1)S(1)}, bf16[4,16,32,128]{3,2,1,0:T(8,128)(2,1)S(1)}, bf16[4,128,1024]{2,1,0:T(8,128)(2,1)S(1)}) custom-call(s32[1,128]{1,0:T(1,128)S(1)} %copy-done.5, bf16[128,4096]{1,0:T(8,128)(2,1)S(1)} %copy-done.2, bf16[128,2048]{1,0:T(8,128)(2,1)S(1)} %copy-done.3, ...), custom_call_target="tpu_custom_call" | custom-call | tf_op jit(solution)/shard_map/project/pallas_call | solution.py:78
  12.3 45.0 %spread.1 = (bf16[4,4,16,16,128]{4,3,2,1,0:T(8,128)(2,1)S(1)}, bf16[4,16,32,128]{3,2,1,0:T(8,128)(2,1)S(1)}, bf16[4,16,32,128]{3,2,1,0:T(8,128)(2,1)S(1)}, bf16[4,128,1024]{2,1,0:T(8,128)(2,1)S(1)}) custom-call(bf16[16,64,128]{2,1,0:T(8,128)(2,1)S(1)} %get-tuple-element.22.kv_s, bf16[16,128,128]{2,1,0:T(8,128)(2,1)S(1)} %get-tuple-element.23.q_s, ...), custom_call_target="tpu_custom_call" | custom-call | tf_op jit(solution)/shard_map/spread/pallas_call | solution.py:187
  57.3 0.0 copy-done.6
  57.3 0.6 convert_reduce_fusion
  57.9 0.1 broadcast_in_dim.7
  58.1 0.2 reshape.60.first
  58.2 0.1 slice.3
  58.3 0.1 pad_add_fusion.info
  58.4 6.3 %attend.1 = (bf16[2048,128]{1,0:T(8,128)(2,1)S(1)}, bf16[2048,128]{1,0:T(8,128)(2,1)S(1)}, bf16[4,2,512,128]{3,2,1,0:T(8,128)(2,1)S(1)}) custom-call(s32[5]{0:T(128)S(1)} %pad_add_fusion.info, bf16[2048,128]{1,0:T(8,128)(2,1)S(1)} %bitcast.13, bf16[2048,128]{1,0:T(8,128)(2,1)S(1)} %bitcast.14, bf16[256,16,128]{2,1,0:T(8,128)(2,1)S(1)} %bitcast.11, ...), custom_call_target="tpu_custom_call" | custom-call | tf_op jit(solution)/shard_map/attend/pallas_call | solution.py:296
  64.8 1.0 fusion
  65.7 0.2 pad_maximum_fusion
  66.0 53.9 %collect.1 = (bf16[4,512,128]{2,1,0:T(8,128)(2,1)S(1)}, bf16[4,512,128]{2,1,0:T(8,128)(2,1)S(1)}, bf16[4,16,16,128]{3,2,1,0:T(8,128)(2,1)S(1)}, bf16[4,16,4,16,128]{4,3,2,1,0:T(8,128)(2,1)S(1)}) custom-call(bf16[4,512,128]{2,1,0:T(8,128)(2,1)S(1)} %bitcast.15, bf16[4,512,128]{2,1,0:T(8,128)(2,1)S(1)} %bitcast.16, ...), custom_call_target="tpu_custom_call" | custom-call | tf_op jit(solution)/shard_map/collect/pallas_call | solution.py:392
  119.8 2.5 %weight.1 = bf16[16,4,64,256]{3,2,1,0:T(8,128)(2,1)S(1)} custom-call(bf16[4,16,4,16,128]{4,3,2,1,0:T(8,128)(2,1)S(1)} %get-tuple-element.38.src, bf16[512,1024]{1,0:T(8,128)(2,1)S(1)} %bitcast.12), custom_call_target="tpu_custom_call" | custom-call | tf_op jit(solution)/shard_map/weight/pallas_call | solution.py:437
  122.3 28.8 %reduce_tiles.1 = f32[64,256]{1,0:T(8,128)S(1)} custom-call(bf16[2,4,2,4,64,256]{5,4,3,2,1,0:T(8,128)(2,1)S(1)} %bitcast.10), custom_call_target="tpu_custom_call" | custom-call | tf_op jit(solution)/shard_map/reduce_tiles/pallas_call | solution.py:504
  151.1 0.0 copy-start.1
  151.1 3.4 %copy-done.1 = bf16[1024,4096]{1,0:T(8,128)(2,1)S(1)} copy-done((bf16[1024,4096]{1,0:T(8,128)(2,1)S(1)}, bf16[1024,4096]{1,0:T(8,128)(2,1)}, u32[]{:S(2)}) %copy-start.1) | copy-done | bytes 8388632
  154.5 5.0 %finish.1 = (bf16[128,2048]{1,0:T(8,128)(2,1)}, bf16[128,2048]{1,0:T(8,128)(2,1)}, bf16[128,4096]{1,0:T(8,128)(2,1)}) custom-call(bf16[4,512,128]{2,1,0:T(8,128)(2,1)S(1)} %get-tuple-element.32.att, bf16[4,512,128]{2,1,0:T(8,128)(2,1)S(1)} %get-tuple-element.33.qg, bf16[4,16,16,128]{3,2,1,0:T(8,128)(2,1)S(1)} %get-tuple-element.34.pg, ...), custom_call_target="tpu_custom_call" | custom-call | tf_op jit(solution)/shard_map/finish/pallas_call | solution.py:550
  159.5 0.6 copy.13
  (5 shorter events, 0.1 us)
Async XLA Ops:
  0.9 3.4 %copy-start = (bf16[1024,4096]{1,0:T(8,128)(2,1)S(1)}, bf16[1024,4096]{1,0:T(8,128)(2,1)}, u32[]{:S(2)}) copy-start(bf16[1024,4096]{1,0:T(8,128)(2,1)} %w2.1) | copy-start | bytes 25165828
  4.2 1.2 copy-start.2
  5.5 1.0 copy-start.3
  6.5 1.0 copy-start.4
  7.6 0.7 copy-start.5
  8.2 49.1 %copy-start.6 = (s32[1,2048]{1,0:T(1,128)S(1)}, s32[1,2048]{1,0:T(1,128)}, u32[]{:S(2)}) copy-start(s32[1,2048]{1,0:T(1,128)} %param.11) | copy-start | bytes 24580
  151.1 3.4 %copy-start.1 = (bf16[1024,4096]{1,0:T(8,128)(2,1)S(1)}, bf16[1024,4096]{1,0:T(8,128)(2,1)}, u32[]{:S(2)}) copy-start(bf16[1024,4096]{1,0:T(8,128)(2,1)} %w2.1) | copy-start | bytes 25165828

commit v3 on v2

v3 whole, which is shorter than its diff:
```python
import functools
import math

import jax
import jax.numpy as jnp
from jax import lax
from jax.experimental import pallas as pl
from jax.experimental.pallas import tpu as pltpu
from jax.sharding import PartitionSpec as P

ROPE_BASE = 500000.0
MASK_VALUE = -1e30
HD = 128
SCALE = HD ** (-0.5)
BF = jnp.bfloat16
F32 = jnp.float32
MESH = pl.DeviceIdType.MESH
KB = 256
MIB = 1024 * 1024


def vm():
    return pl.BlockSpec(memory_space=pltpu.VMEM)


def rows_dot(a, b):
    return lax.dot_general(a, b, (((1,), (1,)), ((), ())), preferred_element_type=F32)


def cols_dot(a, b):
    return lax.dot_general(a, b, (((0,), (0,)), ((), ())), preferred_element_type=F32)


def angle_tables(positions):
    half = HD // 2
    exponent = jnp.arange(half, dtype=F32) * (-2.0 * math.log(ROPE_BASE) / HD)
    angles = positions.astype(F32)[:, None] * jnp.exp(exponent)[None, :]
    cosine, sine = jnp.cos(angles), jnp.sin(angles)
    return jnp.concatenate([cosine, cosine], 1), jnp.concatenate([-sine, sine], 1)


def remote(src, dst, send, recv, device):
    return pltpu.make_async_remote_copy(
        src_ref=src, dst_ref=dst, send_sem=send, recv_sem=recv, device_id=device, device_id_type=MESH
    )


def greet(devices):
    barrier = pltpu.get_barrier_semaphore()
    for device in devices:
        pl.semaphore_signal(barrier, inc=1, device_id=device, device_id_type=MESH)
    pl.semaphore_wait(barrier, len(devices))


def front_kernel(
    plan, cos, sin, x_h, q_h, og_h, w_h, kv_all, q_rx, g_rx, h_rx,
    x, q, og, w, xp, acc, kv_s, q_s, g_s, h_s, kv1, q1, ls, ss, rs, ys, yr, zs, zr,
):
    d, c = lax.axis_index("dp"), lax.axis_index("ctx")
    z, y = c // 4, c % 4
    dp_of = [(d + k) % 16 for k in range(16)]
    y_of = [(y + k) % 4 for k in range(4)]
    on_dp = lambda k: {"dp": dp_of[k]}
    on_y = lambda k: {"ctx": z * 4 + y_of[k]}
    up, down = {"ctx": (c + 4) % 16}, {"ctx": (c + 12) % 16}
    z_up, z_down = (z + 1) % 4, (z + 3) % 4

    loads = [
        pltpu.make_async_copy(og_h, og, ls.at[0]),
        pltpu.make_async_copy(q_h, q, ls.at[1]),
        pltpu.make_async_copy(x_h, x, ls.at[2]),
    ]
    loads += [pltpu.make_async_copy(w_h.at[pl.ds(i * 256, 256)], w.at[i], ls.at[3 + i]) for i in range(4)]
    for copy in loads:
        copy.start()
    partners = [on_dp(k) for k in range(1, 16)] + [on_y(k) for k in range(1, 4)] + [up, down]
    barrier = pltpu.get_barrier_semaphore()
    for device in partners:
        pl.semaphore_signal(barrier, inc=1, device_id=device, device_id_type=MESH)

    loads[0].wait()
    for i in range(8):
        grads = [og[:, h * HD : (h + 1) * HD].astype(F32).reshape(16, 8, HD) for h in (2 * i, 2 * i + 1)]
        g_s[i // 2, :, (i % 2) * 16 : (i % 2 + 1) * 16, :] = jnp.concatenate(grads, 1).astype(BF)
    pl.semaphore_wait(barrier, len(partners))
    grads = [remote(g_s.at[y_of[k]], g_rx.at[y], ys.at[0, k], yr.at[0, k], on_y(k)) for k in range(1, 4)]
    for copy in grads:
        copy.start()

    pick = (lax.broadcasted_iota(jnp.int32, (128, 128), 0) == plan[...]).astype(F32).astype(BF)
    loads[1].wait()
    for i in range(8):
        parts = [
            jnp.dot(pick, q[:, h * HD : (h + 1) * HD], preferred_element_type=F32).reshape(16, 8, HD)
            for h in (2 * i, 2 * i + 1)
        ]
        q_s[:, i * 16 : (i + 1) * 16, :] = jnp.concatenate(parts, 1).astype(BF)
    q_first = [remote(q_s.at[dp_of[k]], q1.at[d], ss.at[1, k], rs.at[1, k], on_dp(k)) for k in range(1, 16)]
    for copy in q_first:
        copy.start()

    loads[2].wait()
    for j in range(16):
        sl = slice(j * 256, (j + 1) * 256)
        t = jnp.dot(pick, x[:, sl], preferred_element_type=F32).astype(BF)
        xp[:, sl] = t
        h_s[j % 4, :, (j // 4) * 256 : (j // 4 + 1) * 256] = t
    for i in range(4):
        loads[3 + i].wait()
        acc[i] = rows_dot(xp[...], w[i])
    for g in range(4):
        sl = slice((g % 2) * HD, (g % 2 + 1) * HD)
        k = acc[g // 2][:, sl]
        v = acc[2 + g // 2][:, sl]
        k3 = k.reshape(16, 8, HD)
        r3 = pltpu.roll(k, 64, 1).reshape(16, 8, HD)
        rot = k3 * cos[...][None] + r3 * sin[...][None]
        kv_s[:, g * 16 : (g + 1) * 16, :] = jnp.concatenate([rot, v.reshape(16, 8, HD)], 1).astype(BF)
    kv_first = [remote(kv_s.at[dp_of[k]], kv1.at[d], ss.at[0, k], rs.at[0, k], on_dp(k)) for k in range(1, 16)]
    for copy in kv_first:
        copy.start()
    kv1[d] = kv_s[d]
    q1[d] = q_s[d]
    g_rx[y] = g_s[y]
    h_rx[y] = h_s[y]

    for copy in q_first:
        copy.wait_recv()
    heads = lambda k: pl.ds(pl.multiple_of(y_of[k] * 32, 32), 32)
    q_second = [remote(q1.at[:, heads(k), :], q_rx.at[y], ys.at[2, k], yr.at[2, k], on_y(k)) for k in range(1, 4)]
    for copy in q_second:
        copy.start()
    q_rx[y] = q1[:, heads(0), :]

    for copy in kv_first:
        copy.wait_recv()
    group = lambda k: pl.ds(pl.multiple_of(y_of[k] * 16, 16), 16)
    kv_second = [
        remote(kv1.at[:, group(k), :], kv_all.at[z, y], ys.at[1, k], yr.at[1, k], on_y(k)) for k in range(1, 4)
    ]
    for copy in kv_second:
        copy.start()
    kv_all[z, y] = kv1[:, group(0), :]

    chunk = [(y + 4 - t) % 4 for t in range(4)]
    own_up, own_down = [], []
    for t in range(4):
        if t:
            kv_second[t - 1].wait_recv()
        place = kv_all.at[z, chunk[t]]
        own_up.append(remote(place, place, zs.at[0, t], zr.at[0, t], up))
        own_down.append(remote(place, place, zs.at[1, t], zr.at[1, t], down))
        own_up[t].start()
        own_down[t].start()
    hidden = [remote(h_s.at[y_of[k]], h_rx.at[y], ys.at[3, k], yr.at[3, k], on_y(k)) for k in range(1, 4)]
    for copy in hidden:
        copy.start()

    passed = []
    for t in range(4):
        if t % 2 == 0:
            own_up[t].wait_recv()
            place = kv_all.at[z_down, chunk[t]]
            passed.append(remote(place, place, zs.at[2, t], zr.at[2, t], up))
        else:
            own_down[t].wait_recv()
            place = kv_all.at[z_up, chunk[t]]
            passed.append(remote(place, place, zs.at[2, t], zr.at[2, t], down))
        passed[t].start()
    for t in range(4):
        (own_down if t % 2 == 0 else own_up)[t].wait_recv()
    for copy in passed + q_second + grads + hidden:
        copy.wait_recv()
    for copy in kv_first + grads + q_first + kv_second + own_up + own_down + q_second + hidden + passed:
        copy.wait_send()


def front(plan, cos, sin, x, q, og, w):
    hbm = pl.BlockSpec(memory_space=pltpu.HBM)
    return pl.pallas_call(
        front_kernel,
        in_specs=[vm()] * 3 + [hbm] * 4,
        out_specs=[vm()] * 4,
        out_shape=[
            jax.ShapeDtypeStruct((4, 4, 16, 16, HD), BF),
            jax.ShapeDtypeStruct((4, 16, 32, HD), BF),
            jax.ShapeDtypeStruct((4, 16, 32, HD), BF),
            jax.ShapeDtypeStruct((4, 128, 1024), BF),
        ],
        scratch_shapes=[
            pltpu.VMEM((128, 4096), BF),
            pltpu.VMEM((128, 2048), BF),
            pltpu.VMEM((128, 2048), BF),
            pltpu.VMEM((4, 256, 4096), BF),
            pltpu.VMEM((128, 4096), BF),
            pltpu.VMEM((4, 128, 256), F32),
            pltpu.VMEM((16, 64, HD), BF),
            pltpu.VMEM((16, 128, HD), BF),
            pltpu.VMEM((4, 16, 32, HD), BF),
            pltpu.VMEM((4, 128, 1024), BF),
            pltpu.VMEM((16, 64, HD), BF),
            pltpu.VMEM((16, 128, HD), BF),
            pltpu.SemaphoreType.DMA((7,)),
            pltpu.SemaphoreType.DMA((2, 16)),
            pltpu.SemaphoreType.DMA((2, 16)),
            pltpu.SemaphoreType.DMA((4, 4)),
            pltpu.SemaphoreType.DMA((4, 4)),
            pltpu.SemaphoreType.DMA((3, 4)),
            pltpu.SemaphoreType.DMA((3, 4)),
        ],
        compiler_params=pltpu.CompilerParams(collective_id=0, has_side_effects=True, vmem_limit_bytes=40 * MIB),
        name="front",
    )(plan, cos, sin, x, q, og, w)


def attend_kernel(info, q, og, kv, first, att, qg, dkv, keys, vals, keys_t, vals_t, dk, dv, sc, gp, q_t, og_t, out_t, grad_t):
    base = info[0]
    for i in range(4):
        block = kv[pl.ds(i * 64, 64)].astype(F32)
        rows = slice(i * 512, (i + 1) * 512)
        k = block[:, :8, :].reshape(512, HD)
        v = block[:, 8:, :].reshape(512, HD)
        keys[rows, :] = k.astype(BF)
        vals[rows, :] = v.astype(BF)
        keys_t[:, rows] = k.T.astype(BF)
        vals_t[:, rows] = v.T.astype(BF)
    keys[2048:, :] = jnp.zeros((128, HD), BF)
    vals[2048:, :] = jnp.zeros((128, HD), BF)
    keys_t[:, 2048:] = jnp.zeros((HD, 128), BF)
    vals_t[:, 2048:] = jnp.zeros((HD, 128), BF)
    dk[...] = jnp.zeros_like(dk)
    dv[...] = jnp.zeros_like(dv)
    fold = SCALE * math.log2(math.e)

    def query_block(qb, carry):
        here = pl.ds(pl.multiple_of(qb * 512, 512), 512)
        q_t[...] = q[here, :].astype(F32).T.astype(BF)
        og_t[...] = og[here, :].astype(F32).T.astype(BF)
        start = (info[1 + qb] // 128) * 128
        count = (base + (qb + 1) * 128 - start + KB - 1) // KB
        lane = lax.broadcasted_iota(jnp.int32, (1, 512), 1)
        position = base + qb * 128 + (lane // 32) * 8 + lane % 8
        lowest = first[qb]
        out_t[...] = jnp.zeros_like(out_t)
        grad_t[...] = jnp.zeros_like(grad_t)

        def eights(t):
            return t.reshape(KB // 8, 8, 512)

        def scores(i, top):
            at = pl.multiple_of(start + i * KB, 128)
            rows = pl.ds(at, KB)
            s = jnp.dot(keys[rows, :], q_t[...], preferred_element_type=F32)
            index = at + lax.broadcasted_iota(jnp.int32, (KB, 512), 0)
            s = jnp.where((index <= position) & (index >= lowest), s, MASK_VALUE)
            sc[rows, :] = s
            return jnp.maximum(top, jnp.max(eights(s), axis=0))

        top = lax.fori_loop(0, count, scores, jnp.full((8, 512), MASK_VALUE, F32))
        top = jnp.max(top, axis=0, keepdims=True) * fold

        def expo(i, sums):
            rows = pl.ds(pl.multiple_of(start + i * KB, 128), KB)
            e = jnp.exp2(sc[rows, :] * fold - top)
            grad = jnp.dot(vals[rows, :], og_t[...], preferred_element_type=F32)
            sc[rows, :] = e
            gp[rows, :] = grad
            return sums[0] + jnp.sum(eights(e), axis=0), sums[1] + jnp.sum(eights(e * grad), axis=0)

        zero = jnp.zeros((8, 512), F32)
        total, product = lax.fori_loop(0, count, expo, (zero, zero))
        inverse = 1.0 / jnp.sum(total, axis=0, keepdims=True)
        delta = jnp.sum(product, axis=0, keepdims=True) * inverse

        def both(i, c):
            at = pl.multiple_of(start + i * KB, 128)
            rows = pl.ds(at, KB)
            p = sc[rows, :] * inverse
            rounded = p.astype(BF)
            ds = (p * (gp[rows, :] - delta)).astype(BF)
            dv[rows, :] += jnp.dot(rounded, og[here, :], preferred_element_type=F32)
            dk[rows, :] += jnp.dot(ds, q[here, :], preferred_element_type=F32)
            out_t[...] += jnp.dot(vals_t[:, rows], rounded, preferred_element_type=F32)
            grad_t[...] += jnp.dot(keys_t[:, rows], ds, preferred_element_type=F32)
            return c

        lax.fori_loop(0, count, both, 0)
        att[here, :] = out_t[...].T.astype(BF)
        qg[here, :] = (grad_t[...] * SCALE).T.astype(BF)
        return carry

    lax.fori_loop(0, 4, query_block, 0)
    for i in range(4):
        rows = slice(i * 512, (i + 1) * 512)
        dkv[i, 0] = (dk[rows, :] * SCALE).astype(BF)
        dkv[i, 1] = dv[rows, :].astype(BF)


def attend(info, q, og, kv, first):
    return pl.pallas_call(
        attend_kernel,
        in_specs=[pl.BlockSpec(memory_space=pltpu.SMEM)] + [vm()] * 4,
        out_specs=[vm()] * 3,
        scratch_shapes=[
            pltpu.VMEM((2176, HD), BF),
            pltpu.VMEM((2176, HD), BF),
            pltpu.VMEM((HD, 2176), BF),
            pltpu.VMEM((HD, 2176), BF),
            pltpu.VMEM((2176, HD), F32),
            pltpu.VMEM((2176, HD), F32),
            pltpu.VMEM((2176, 512), F32),
            pltpu.VMEM((2176, 512), F32),
            pltpu.VMEM((HD, 512), BF),
            pltpu.VMEM((HD, 512), BF),
            pltpu.VMEM((HD, 512), F32),
            pltpu.VMEM((HD, 512), F32),
        ],
        out_shape=[
            jax.ShapeDtypeStruct((2048, HD), BF),
            jax.ShapeDtypeStruct((2048, HD), BF),
            jax.ShapeDtypeStruct((4, 2, 512, HD), BF),
        ],
        compiler_params=pltpu.CompilerParams(vmem_limit_bytes=48 * MIB),
        name="attend",
    )(info, q, og, kv, first)


def back_kernel(
    att, qg, dkv, cos, sin, hs, w_h, att_o, qg_o, hg_o, grad,
    att_rx, qg_rx, hop, mid, fin, own_a, own_b, src, pg_rx, hsr, pgh, w, tile, pair, mine, ring, part, last,
    ws, ys, yr, zs, zr, ss, rs, cs, cr, xs, xr, es, er,
):
    d, c = lax.axis_index("dp"), lax.axis_index("ctx")
    z, y = c // 4, c % 4
    zl, x, core = d // 8, (d // 2) % 4, d % 2
    dp_of = [(d + k) % 16 for k in range(16)]
    y_of = [(y + k) % 4 for k in range(4)]
    x_of = [(x + k) % 4 for k in range(4)]
    z_of = [(z + k) % 4 for k in range(4)]
    on_dp = lambda k: {"dp": dp_of[k]}
    on_y = lambda k: {"ctx": z * 4 + y_of[k]}
    on_x = lambda k: {"dp": zl * 8 + x_of[k] * 2 + core}
    on_z = lambda lo, k: {"dp": lo * 8 + x * 2 + core, "ctx": z_of[k] * 4 + y}
    sibling = {"dp": d + 1 - 2 * core}
    up, down = {"ctx": (c + 4) % 16}, {"ctx": (c + 12) % 16}
    z_up, z_far, z_down = z_of[1], z_of[2], z_of[3]
    low, high = pl.ds(0, 256), pl.ds(256, 256)

    weights = pltpu.make_async_copy(w_h, w, ws)
    weights.start()
    greet(
        [on_dp(k) for k in range(1, 16)]
        + [on_y(k) for k in range(1, 4)]
        + [on_z(zl, k) for k in range(1, 4)]
        + [on_z(1 - zl, k) for k in range(1, 4)]
    )

    far, near = {}, {}
    for s in (1, 0):
        far[s] = [
            remote(dkv.at[z_far, s, low], hop.at[s, 0], zs.at[s, 0], zr.at[s, 0], down),
            remote(dkv.at[z_far, s, high], hop.at[s, 1], zs.at[s, 1], zr.at[s, 1], up),
        ]
        near[s] = [
            remote(dkv.at[z_down, s, high], fin.at[s, 0, high], zs.at[s, 2], zr.at[s, 2], down),
            remote(dkv.at[z_up, s, low], fin.at[s, 0, low], zs.at[s, 3], zr.at[s, 3], up),
        ]
        for copy in far[s] + near[s]:
            copy.start()
    outs = []
    for i, (a, b) in enumerate(((att, att_rx), (qg, qg_rx))):
        for k in range(1, 4):
            outs.append(remote(a.at[y_of[k]], b.at[y], ys.at[i, k], yr.at[i, k], on_y(k)))
            outs[-1].start()
        b[y] = a[y]

    sums = {}

    def pass_on(s):
        far[s][0].wait_recv()
        mid[s, 0] = (hop[s, 0].astype(F32) + dkv[z_down, s, 0:256, :].astype(F32)).astype(BF)
        first = remote(mid.at[s, 0], fin.at[s, 1, low], zs.at[s, 4], zr.at[s, 4], down)
        first.start()
        far[s][1].wait_recv()
        mid[s, 1] = (hop[s, 1].astype(F32) + dkv[z_up, s, 256:512, :].astype(F32)).astype(BF)
        second = remote(mid.at[s, 1], fin.at[s, 1, high], zs.at[s, 5], zr.at[s, 5], up)
        second.start()
        sums[s] = [first, second]

    exchanged, packed = {}, {}

    def complete(s):
        for copy in near[s] + sums[s]:
            copy.wait_recv()
        for i in range(2):
            pieces = []
            for j in (2 * i, 2 * i + 1):
                sl = slice(j * 128, (j + 1) * 128)
                t = dkv[z, s, sl, :].astype(F32) + fin[s, 0, sl, :].astype(F32) + fin[s, 1, sl, :].astype(F32)
                t = t.astype(BF).astype(F32)
                if s == 0:
                    t = t * cos[sl, :] - pltpu.roll(t, 64, 1) * sin[sl, :]
                own_b[s, j] = t.astype(BF)
                pieces.append(t.reshape(16, 8, HD))
            own_a[s, :, i * 16 : (i + 1) * 16, :] = jnp.concatenate(pieces, 1).astype(BF)
        exchanged[s] = [
            remote(own_a.at[s, dp_of[k]], src.at[s, y, d], ss.at[s, k], rs.at[s, k], on_dp(k)) for k in range(1, 16)
        ]
        for copy in exchanged[s]:
            copy.start()
        packed[s] = [
            remote(own_b.at[s, y_of[k]], pg_rx.at[s, y], ys.at[2 + s, k], yr.at[2 + s, k], on_y(k))
            for k in range(1, 4)
        ]
        for copy in packed[s]:
            copy.start()
        src[s, y, d] = own_a[s, d]
        pg_rx[s, y] = own_b[s, y]

    gathered = {}

    def gather(s):
        for copy in exchanged[s]:
            copy.wait_recv()
        gathered[s] = [
            remote(src.at[s, y], src.at[s, y], ys.at[4 + s, k], yr.at[4 + s, k], on_y(k)) for k in range(1, 4)
        ]
        for copy in gathered[s]:
            copy.start()

    swaps = {0: [], 1: []}
    order = [2, 1, 3, 0]

    def multiply(s):
        for copy in gathered[s]:
            copy.wait_recv()
        for k in order:
            g = x_of[k]
            rows = src[s, g].reshape(512, HD)
            for j in range(4):
                sl = slice(j * 256, (j + 1) * 256)
                tile[s, k, :, :, sl] = cols_dot(rows, hsr[:, sl]).reshape(2, 64, 256).astype(BF)
            copy = remote(tile.at[s, k, 1 - core], pair.at[s, k], cs.at[s, k], cr.at[s, k], sibling)
            copy.start()
            swaps[s].append(copy)

    rings = {0: [], 1: []}

    def add_pair(s):
        for copy, k in zip(swaps[s], order):
            copy.wait_recv()
            for j in range(4):
                sl = slice(j * 256, (j + 1) * 256)
                mine[s, k, :, sl] = (
                    tile[s, k, core, :, sl].astype(F32) + pair[s, k, :, sl].astype(F32)
                ).astype(BF)
            if k:
                copy = remote(mine.at[s, k], ring.at[s, k], xs.at[s, k], xr.at[s, k], on_x(k))
                copy.start()
                rings[s].append(copy)

    same = lambda s, k: remote(part.at[s, z_of[k]], last.at[k], es.at[k], er.at[k], on_z(s, k))
    other = lambda s, k: remote(part.at[s, z_of[k]], last.at[4 + k], es.at[4 + k], er.at[4 + k], on_z(s, k))

    def add_ring(s):
        for copy in rings[s]:
            copy.wait_recv()
        for j in range(4):
            sl = slice(j * 256, (j + 1) * 256)
            t = mine[s, 0, :, sl].astype(F32)
            for k in range(1, 4):
                t = t + ring[s, k, :, sl].astype(F32)
            part[s, j] = t.astype(BF)

        @pl.when(zl == s)
        def _():
            for k in range(1, 4):
                same(s, k).start()

        @pl.when(zl != s)
        def _():
            for k in range(4):
                other(s, k).start()

    for j in range(4):
        sl = slice(j * 256, (j + 1) * 256)
        pieces = [hs[i, :, sl].astype(F32).reshape(16, 8, 256) for i in range(4)]
        hsr[:, sl] = jnp.concatenate(pieces, 1).reshape(512, 256).astype(BF)
    pass_on(1)
    pass_on(0)
    complete(1)
    for copy in outs:
        copy.wait_recv()
    for g in range(4):
        for source, target in ((att_rx, att_o), (qg_rx, qg_o)):
            block = source[g].reshape(16, 32, HD).astype(F32)
            for h in range(4):
                cols = slice((g * 4 + h) * HD, (g * 4 + h + 1) * HD)
                target[:, cols] = block[:, h * 8 : h * 8 + 8, :].reshape(128, HD).astype(BF)
    gather(1)
    complete(0)
    multiply(1)
    gather(0)
    add_pair(1)
    multiply(0)
    add_ring(1)
    for s in (1, 0):
        for copy in packed[s]:
            copy.wait_recv()
        for g in range(4):
            cols = slice(s * 512 + g * HD, s * 512 + (g + 1) * HD)
            pgh[:, cols] = pg_rx[s, g]
    add_pair(0)
    weights.wait()
    for j in range(8):
        sl = slice(j * 512, (j + 1) * 512)
        hg_o[:, sl] = jnp.dot(pgh[...], w[:, sl], preferred_element_type=F32).astype(BF)
    add_ring(0)
    ends = [same(zl, k) for k in range(1, 4)] + [other(1 - zl, k) for k in range(4)]
    for copy in ends:
        copy.wait_recv()
    t = part[zl, z].astype(F32)
    for k in range(1, 8):
        t = t + last[k].astype(F32)
    grad[...] = t * (1.0 / 16.0)
    for s in (0, 1):
        for copy in far[s] + near[s] + sums[s] + exchanged[s] + packed[s] + gathered[s] + swaps[s] + rings[s]:
            copy.wait_send()
    for copy in outs + ends:
        copy.wait_send()


def back(att, qg, dkv, cos, sin, hs, w):
    dma = pltpu.SemaphoreType.DMA
    return pl.pallas_call(
        back_kernel,
        in_specs=[vm()] * 6 + [pl.BlockSpec(memory_space=pltpu.HBM)],
        out_specs=[vm()] * 4,
        out_shape=[
            jax.ShapeDtypeStruct((128, 2048), BF),
            jax.ShapeDtypeStruct((128, 2048), BF),
            jax.ShapeDtypeStruct((128, 4096), BF),
            jax.ShapeDtypeStruct((64, 256), F32),
        ],
        scratch_shapes=[
            pltpu.VMEM((4, 512, HD), BF),
            pltpu.VMEM((4, 512, HD), BF),
            pltpu.VMEM((2, 2, 256, HD), BF),
            pltpu.VMEM((2, 2, 256, HD), BF),
            pltpu.VMEM((2, 2, 512, HD), BF),
            pltpu.VMEM((2, 16, 32, HD), BF),
            pltpu.VMEM((2, 4, 128, HD), BF),
            pltpu.VMEM((2, 4, 16, 32, HD), BF),
            pltpu.VMEM((2, 4, 128, HD), BF),
            pltpu.VMEM((512, 1024), BF),
            pltpu.VMEM((128, 1024), BF),
            pltpu.VMEM((1024, 4096), BF),
            pltpu.VMEM((2, 4, 2, 64, 1024), BF),
            pltpu.VMEM((2, 4, 64, 1024), BF),
            pltpu.VMEM((2, 4, 64, 1024), BF),
            pltpu.VMEM((2, 4, 64, 1024), BF),
            pltpu.VMEM((2, 4, 64, 256), BF),
            pltpu.VMEM((8, 64, 256), BF),
            dma, dma((6, 4)), dma((6, 4)), dma((2, 6)), dma((2, 6)), dma((2, 16)), dma((2, 16)),
            dma((2, 4)), dma((2, 4)), dma((2, 4)), dma((2, 4)), dma((8,)), dma((8,)),
        ],
        compiler_params=pltpu.CompilerParams(collective_id=1, has_side_effects=True, vmem_limit_bytes=48 * MIB),
        name="back",
    )(att, qg, dkv, cos, sin, hs, w)


def body(hidden_rows, query_rows, out_grad, projection, packing_plan, document_ids):
    d, c = lax.axis_index("dp"), lax.axis_index("ctx")
    z = c // 4
    near_cos, near_sin = angle_tables(c * 128 + d * 8 + jnp.arange(8, dtype=jnp.int32))
    cos, sin = angle_tables(z * 512 + jnp.arange(512, dtype=jnp.int32))
    documents = document_ids[0]
    own_documents = lax.dynamic_slice_in_dim(documents, z * 512, 512)
    first = jnp.sum((documents[None, :] < own_documents[:, None]).astype(jnp.int32), axis=1)
    info = jnp.concatenate([(z * 512)[None].astype(jnp.int32), first[::128]])
    first_rows = jnp.broadcast_to(first.reshape(64, 1, 8), (64, 4, 8)).reshape(4, 1, 512)

    kv_all, q_rx, g_rx, h_rx = front(
        packing_plan, near_cos, near_sin, hidden_rows, query_rows, out_grad, projection
    )
    att, qg, dkv = attend(
        info, q_rx.reshape(2048, HD), g_rx.reshape(2048, HD), kv_all.reshape(256, 16, HD), first_rows
    )
    attended, query_grad, hidden_grad, weight_grad = back(
        att.reshape(4, 512, HD), qg.reshape(4, 512, HD), dkv, cos, sin, h_rx, projection
    )
    return attended, query_grad, hidden_grad, weight_grad


def solution(mesh):
    rows = P(("dp", "ctx"), None)
    return jax.shard_map(
        body,
        mesh=mesh,
        in_specs=(rows, rows, rows, P(), rows, P("dp", None)),
        out_specs=(rows, rows, rows, P("dp", "ctx")),
        check_vma=False,
    )
```

time: 160 us -> 143 us (0.89)
  Pallas kernels: 146 us -> 127 us
    pallas_call x6 -> x2, Pallas kernels: 139 us -> 121 us  [the longest x1 76 us: back(): pl.pallas_call(back_kernel, in_specs=[vm()] * 6 + [pl.BlockSpec(memory_sp...]
    unnamed x15 -> x14, local copies, waits for them, and re-layouts: 11.4 us -> 10.5 us
where the time goes in v3:
time: 143 us; the launch traced here: 142 us
  Pallas kernels  127 us (89%)
  local copies, waits for them, and re-layouts  11.6 us (8%)
  other arithmetic  2.73 us (2%)
    pallas_call x1, Pallas kernels, back(): pl.pallas_call(back_kernel, in_specs=[vm()] * 6 + [pl.BlockSpec(memory_sp...  76 us
    pallas_call x1, Pallas kernels, front(): pl.pallas_call(front_kernel, in_specs=[vm()] * 3 + [hbm] * 4, out_specs=[...  44.9 us
    unnamed x14, local copies, waits for them, and re-layouts  10.5 us
    pallas_call x1, Pallas kernels, attend(): pl.pallas_call(attend_kernel, in_specs=[pl.BlockSpec(memory_space=pltpu.S...  6.37 us

profile of v3, /device:TPU:1, one launch (start us, length us, event | category | flops | bytes accessed | tf_op | source)
XLA Modules:
  0.0 142.3 jit_solution(14803556443722893133)
XLA Ops:
  0.7 0.7 constant_dynamic-slice_fusion
  1.4 1.3 convert_reduce_fusion
  2.6 0.1 slice.3
  2.7 0.1 pad_add_fusion.info
  2.8 0.1 fusion.1
  2.9 0.1 pad_maximum_fusion.2
  3.0 0.1 broadcast_in_dim.7
  3.1 0.2 reshape.52.first
  3.3 1.0 fusion
  4.3 0.2 pad_maximum_fusion
  4.5 0.0 copy-start
  4.5 3.4 %copy-done = bf16[1024,4096]{1,0:T(8,128)(2,1)S(1)} copy-done((bf16[1024,4096]{1,0:T(8,128)(2,1)S(1)}, bf16[1024,4096]{1,0:T(8,128)(2,1)}, u32[]{:S(2)}) %copy-start) | copy-done | bytes 8388632
  7.9 0.0 copy-start.1
  7.9 1.2 copy-done.1
  9.1 0.0 copy-start.2
  9.1 1.0 copy-done.2
  10.1 0.0 copy-start.3
  10.1 1.0 copy-done.3
  11.2 0.0 copy-start.4
  11.2 0.7 copy-done.4
  11.8 44.9 %front.1 = (bf16[4,4,16,16,128]{4,3,2,1,0:T(8,128)(2,1)S(1)}, bf16[4,16,32,128]{3,2,1,0:T(8,128)(2,1)S(1)}, bf16[4,16,32,128]{3,2,1,0:T(8,128)(2,1)S(1)}, bf16[4,128,1024]{2,1,0:T(8,128)(2,1)S(1)}) custom-call(s32[1,128]{1,0:T(1,128)S(1)} %copy-done.4, f32[8,128]{1,0:T(8,128)S(1)} %get-tuple-element.24.cos, f32[8,128]{1,0:T(8,128)S(1)} %get-tuple-element.25.sin, ...), custom_call_target="tpu_custom_call" | custom-call | tf_op jit(solution)/shard_map/front/pallas_call | solution.py:180
  56.7 6.4 %attend.1 = (bf16[2048,128]{1,0:T(8,128)(2,1)S(1)}, bf16[2048,128]{1,0:T(8,128)(2,1)S(1)}, bf16[4,2,512,128]{3,2,1,0:T(8,128)(2,1)S(1)}) custom-call(s32[5]{0:T(128)S(1)} %pad_add_fusion.info, bf16[2048,128]{1,0:T(8,128)(2,1)S(1)} %bitcast.11, bf16[2048,128]{1,0:T(8,128)(2,1)S(1)} %bitcast.12, bf16[256,16,128]{2,1,0:T(8,128)(2,1)S(1)} %bitcast.8, ...), custom_call_target="tpu_custom_call" | custom-call | tf_op jit(solution)/shard_map/attend/pallas_call | solution.py:300
  63.1 76.0 %back.1 = (bf16[128,2048]{1,0:T(8,128)(2,1)S(1)}, bf16[128,2048]{1,0:T(8,128)(2,1)S(1)}, bf16[128,4096]{1,0:T(8,128)(2,1)S(1)}, f32[64,256]{1,0:T(8,128)S(1)}) custom-call(bf16[4,512,128]{2,1,0:T(8,128)(2,1)S(1)} %bitcast.9, bf16[4,512,128]{2,1,0:T(8,128)(2,1)S(1)} %bitcast.10, bf16[4,2,512,128]{3,2,1,0:T(8,128)(2,1)S(1)} %get-tuple-element.16.dkv, ...), custom_call_target="tpu_custom_call" | custom-call | tf_op jit(solution)/shard_map/back/pallas_call | solution.py:535
  139.1 0.8 copy.16
  139.9 0.8 copy.17
  140.7 1.0 copy.18
  141.7 0.6 copy.19
  (4 shorter events, 0.0 us)
Async XLA Ops:
  4.5 3.4 %copy-start = (bf16[1024,4096]{1,0:T(8,128)(2,1)S(1)}, bf16[1024,4096]{1,0:T(8,128)(2,1)}, u32[]{:S(2)}) copy-start(bf16[1024,4096]{1,0:T(8,128)(2,1)} %w_h.3) | copy-start | bytes 25165828
  7.9 1.2 copy-start.1
  9.1 1.0 copy-start.2
  10.1 1.0 copy-start.3
  11.2 0.7 copy-start.4

commit v4 on v3

--- a/solution.py
+++ b/solution.py
@@ -39,6 +39,11 @@
     return jnp.concatenate([cosine, cosine], 1), jnp.concatenate([-sine, sine], 1)
 
 
+def turn(cos, sin, rows):
+    c, s, c8, s8 = cos[rows, :], sin[rows, :], cos[64:, :], sin[64:, :]
+    return c * c8 - s * s8, s * c8 + c * s8
+
+
 def remote(src, dst, send, recv, device):
     return pltpu.make_async_remote_copy(
         src_ref=src, dst_ref=dst, send_sem=send, recv_sem=recv, device_id=device, device_id_type=MESH
@@ -53,7 +58,7 @@
 
 
 def front_kernel(
-    plan, cos, sin, x_h, q_h, og_h, w_h, kv_all, q_rx, g_rx, h_rx,
+    plan, documents, cos, sin, x_h, q_h, og_h, w_h, kv_all, q_rx, g_rx, h_rx, lowest,
     x, q, og, w, xp, acc, kv_s, q_s, g_s, h_s, kv1, q1, ls, ss, rs, ys, yr, zs, zr,
 ):
     d, c = lax.axis_index("dp"), lax.axis_index("ctx")
@@ -108,13 +113,14 @@
     for i in range(4):
         loads[3 + i].wait()
         acc[i] = rows_dot(xp[...], w[i])
+    near_cos, near_sin = turn(cos, sin, pl.ds(y * 16 + d, 1))
     for g in range(4):
         sl = slice((g % 2) * HD, (g % 2 + 1) * HD)
         k = acc[g // 2][:, sl]
         v = acc[2 + g // 2][:, sl]
         k3 = k.reshape(16, 8, HD)
         r3 = pltpu.roll(k, 64, 1).reshape(16, 8, HD)
-        rot = k3 * cos[...][None] + r3 * sin[...][None]
+        rot = k3 * near_cos[None] + r3 * near_sin[None]
         kv_s[:, g * 16 : (g + 1) * 16, :] = jnp.concatenate([rot, v.reshape(16, 8, HD)], 1).astype(BF)
     kv_first = [remote(kv_s.at[dp_of[k]], kv1.at[d], ss.at[0, k], rs.at[0, k], on_dp(k)) for k in range(1, 16)]
     for copy in kv_first:
@@ -123,6 +129,18 @@
     q1[d] = q_s[d]
     g_rx[y] = g_s[y]
     h_rx[y] = h_s[y]
+
+    lane = lax.broadcasted_iota(jnp.int32, (128, 512), 1)
+    take = (lax.broadcasted_iota(jnp.int32, (128, 512), 0) == (lane // 32) * 8 + lane % 8).astype(F32).astype(BF)
+    ids = documents[...].astype(F32)
+    counts = [jnp.sum((ids < k).astype(F32), axis=1, keepdims=True) for k in range(1, 8)]
+    for i in range(4):
+        mine = documents[:, pl.ds(pl.multiple_of(z * 512 + i * 128, 128), 128)].astype(F32)
+        mine = jnp.dot(jnp.broadcast_to(mine, (16, 128)).astype(BF), take, preferred_element_type=F32)[:1]
+        begin = jnp.zeros((1, 512), F32)
+        for k in range(1, 8):
+            begin = jnp.where(mine == k, counts[k - 1], begin)
+        lowest[i] = begin.astype(jnp.int32)
 
     for copy in q_first:
         copy.wait_recv()
@@ -175,17 +193,18 @@
         copy.wait_send()
 
 
-def front(plan, cos, sin, x, q, og, w):
+def front(plan, documents, cos, sin, x, q, og, w):
     hbm = pl.BlockSpec(memory_space=pltpu.HBM)
     return pl.pallas_call(
         front_kernel,
-        in_specs=[vm()] * 3 + [hbm] * 4,
-        out_specs=[vm()] * 4,
+        in_specs=[vm()] * 4 + [hbm] * 4,
+        out_specs=[vm()] * 5,
         out_shape=[
             jax.ShapeDtypeStruct((4, 4, 16, 16, HD), BF),
             jax.ShapeDtypeStruct((4, 16, 32, HD), BF),
             jax.ShapeDtypeStruct((4, 16, 32, HD), BF),
             jax.ShapeDtypeStruct((4, 128, 1024), BF),
+            jax.ShapeDtypeStruct((4, 1, 512), jnp.int32),
         ],
         scratch_shapes=[
             pltpu.VMEM((128, 4096), BF),
@@ -208,13 +227,13 @@
             pltpu.SemaphoreType.DMA((3, 4)),
             pltpu.SemaphoreType.DMA((3, 4)),
         ],
-        compiler_params=pltpu.CompilerParams(collective_id=0, has_side_effects=True, vmem_limit_bytes=40 * MIB),
+        compiler_params=pltpu.CompilerParams(collective_id=0, has_side_effects=True, vmem_limit_bytes=49 * MIB),
         name="front",
-    )(plan, cos, sin, x, q, og, w)
-
-
-def attend_kernel(info, q, og, kv, first, att, qg, dkv, keys, vals, keys_t, vals_t, dk, dv, sc, gp, q_t, og_t, out_t, grad_t):
-    base = info[0]
+    )(plan, documents, cos, sin, x, q, og, w)
+
+
+def attend_kernel(q, og, kv, first, att, qg, dkv, keys, vals, keys_t, vals_t, dk, dv, sc, gp, q_t, og_t, out_t, grad_t):
+    base = (lax.axis_index("ctx") // 4) * 512
     for i in range(4):
         block = kv[pl.ds(i * 64, 64)].astype(F32)
         rows = slice(i * 512, (i + 1) * 512)
@@ -236,11 +255,11 @@
         here = pl.ds(pl.multiple_of(qb * 512, 512), 512)
         q_t[...] = q[here, :].astype(F32).T.astype(BF)
         og_t[...] = og[here, :].astype(F32).T.astype(BF)
-        start = (info[1 + qb] // 128) * 128
+        lowest = first[qb]
+        start = (jnp.min(lowest) // 128) * 128
         count = (base + (qb + 1) * 128 - start + KB - 1) // KB
         lane = lax.broadcasted_iota(jnp.int32, (1, 512), 1)
         position = base + qb * 128 + (lane // 32) * 8 + lane % 8
-        lowest = first[qb]
         out_t[...] = jnp.zeros_like(out_t)
         grad_t[...] = jnp.zeros_like(grad_t)
 
@@ -296,10 +315,10 @@
         dkv[i, 1] = dv[rows, :].astype(BF)
 
 
-def attend(info, q, og, kv, first):
+def attend(q, og, kv, first):
     return pl.pallas_call(
         attend_kernel,
-        in_specs=[pl.BlockSpec(memory_space=pltpu.SMEM)] + [vm()] * 4,
+        in_specs=[vm()] * 4,
         out_specs=[vm()] * 3,
         scratch_shapes=[
             pltpu.VMEM((2176, HD), BF),
@@ -322,7 +341,7 @@
         ],
         compiler_params=pltpu.CompilerParams(vmem_limit_bytes=48 * MIB),
         name="attend",
-    )(info, q, og, kv, first)
+    )(q, og, kv, first)
 
 
 def back_kernel(
@@ -399,7 +418,13 @@
                 t = dkv[z, s, sl, :].astype(F32) + fin[s, 0, sl, :].astype(F32) + fin[s, 1, sl, :].astype(F32)
                 t = t.astype(BF).astype(F32)
                 if s == 0:
-                    t = t * cos[sl, :] - pltpu.roll(t, 64, 1) * sin[sl, :]
+                    swapped = pltpu.roll(t, 64, 1)
+                    turned = []
+                    for a in range(16):
+                        rows = slice(a * 8, (a + 1) * 8)
+                        c8, s8 = turn(cos, sin, slice(j * 16 + a, j * 16 + a + 1))
+                        turned.append(t[rows, :] * c8 - swapped[rows, :] * s8)
+                    t = jnp.concatenate(turned, 0)
                 own_b[s, j] = t.astype(BF)
                 pieces.append(t.reshape(16, 8, HD))
             own_a[s, :, i * 16 : (i + 1) * 16, :] = jnp.concatenate(pieces, 1).astype(BF)
@@ -497,10 +522,10 @@
             for h in range(4):
                 cols = slice((g * 4 + h) * HD, (g * 4 + h + 1) * HD)
                 target[:, cols] = block[:, h * 8 : h * 8 + 8, :].reshape(128, HD).astype(BF)
+    complete(0)
     gather(1)
-    complete(0)
+    gather(0)
     multiply(1)
-    gather(0)
     add_pair(1)
     multiply(0)
     add_ring(1)
@@ -569,27 +594,38 @@
     )(att, qg, dkv, cos, sin, hs, w)
 
 
+def store_kernel(a, b, c, e, a_o, b_o, c_o, e_o, sems):
+    copies = [pltpu.make_async_copy(p, o, sems.at[i]) for i, (p, o) in enumerate(((a, a_o), (b, b_o), (c, c_o), (e, e_o)))]
+    for copy in copies:
+        copy.start()
+    for copy in copies:
+        copy.wait()
+
+
+def store(*arrays):
+    hbm = pl.BlockSpec(memory_space=pltpu.HBM)
+    return pl.pallas_call(
+        store_kernel,
+        in_specs=[vm()] * 4,
+        out_specs=[hbm] * 4,
+        out_shape=[jax.ShapeDtypeStruct(a.shape, a.dtype) for a in arrays],
+        scratch_shapes=[pltpu.SemaphoreType.DMA((4,))],
+        compiler_params=pltpu.CompilerParams(vmem_limit_bytes=16 * MIB),
+        name="store",
+    )(*arrays)
+
+
 def body(hidden_rows, query_rows, out_grad, projection, packing_plan, document_ids):
-    d, c = lax.axis_index("dp"), lax.axis_index("ctx")
-    z = c // 4
-    near_cos, near_sin = angle_tables(c * 128 + d * 8 + jnp.arange(8, dtype=jnp.int32))
-    cos, sin = angle_tables(z * 512 + jnp.arange(512, dtype=jnp.int32))
-    documents = document_ids[0]
-    own_documents = lax.dynamic_slice_in_dim(documents, z * 512, 512)
-    first = jnp.sum((documents[None, :] < own_documents[:, None]).astype(jnp.int32), axis=1)
-    info = jnp.concatenate([(z * 512)[None].astype(jnp.int32), first[::128]])
-    first_rows = jnp.broadcast_to(first.reshape(64, 1, 8), (64, 4, 8)).reshape(4, 1, 512)
-
-    kv_all, q_rx, g_rx, h_rx = front(
-        packing_plan, near_cos, near_sin, hidden_rows, query_rows, out_grad, projection
+    z = lax.axis_index("ctx") // 4
+    small = jnp.arange(8, dtype=jnp.int32)
+    cos, sin = angle_tables(jnp.concatenate([z * 512 + jnp.arange(64, dtype=jnp.int32) * 8, small]))
+    kv_all, q_rx, g_rx, h_rx, first = front(
+        packing_plan, document_ids, cos, sin, hidden_rows, query_rows, out_grad, projection
     )
     att, qg, dkv = attend(
-        info, q_rx.reshape(2048, HD), g_rx.reshape(2048, HD), kv_all.reshape(256, 16, HD), first_rows
+        q_rx.reshape(2048, HD), g_rx.reshape(2048, HD), kv_all.reshape(256, 16, HD), first
     )
-    attended, query_grad, hidden_grad, weight_grad = back(
-        att.reshape(4, 512, HD), qg.reshape(4, 512, HD), dkv, cos, sin, h_rx, projection
-    )
-    return attended, query_grad, hidden_grad, weight_grad
+    return store(*back(att.reshape(4, 512, HD), qg.reshape(4, 512, HD), dkv, cos, sin, h_rx, projection))
 
 
 def solution(mesh):

time: 143 us -> 134 us (0.937)
  local copies, waits for them, and re-layouts: 11.6 us -> 3.43 us
  other arithmetic: 2.73 us -> 0.39 us
  Pallas kernels: 127 us -> 129 us
    unnamed x14 -> x8, local copies, waits for them, and re-layouts: 10.5 us -> 3.43 us
    pallas_call x2 -> x3, Pallas kernels: 51.2 us -> 52.8 us  [the longest x1 44.5 us: front(): pl.pallas_call(front_kernel, in_specs=[vm()] * 4 + [hbm] * 4, out_specs=[...]
where the time goes in v4:
time: 134 us
  Pallas kernels  129 us (96%)
  local copies, waits for them, and re-layouts  3.43 us (3%)
    pallas_call x1, Pallas kernels, back(): pl.pallas_call(back_kernel, in_specs=[vm()] * 6 + [pl.BlockSpec(memory_sp...  76.2 us
    pallas_call x1, Pallas kernels, front(): pl.pallas_call(front_kernel, in_specs=[vm()] * 4 + [hbm] * 4, out_specs=[...  44.5 us
    pallas_call x1, Pallas kernels, attend(): pl.pallas_call(attend_kernel, in_specs=[vm()] * 4, out_specs=[vm()] * 3,...  6.97 us
    unnamed x8, local copies, waits for them, and re-layouts  3.43 us

profile of v4, /device:TPU:1, one launch (start us, length us, event | category | flops | bytes accessed | tf_op | source)
XLA Modules:
  0.0 133.6 jit_solution(9582941019631969245)
XLA Ops:
  0.7 0.1 add_convert_fusion
  0.8 0.2 fusion
  1.0 0.1 pad_maximum_fusion
  1.1 0.0 copy-start
  1.1 1.0 copy-done
  2.1 0.0 copy-start.1
  2.1 1.0 copy-done.1
  3.2 0.0 copy-start.2
  3.2 0.7 copy-done.2
  3.9 0.0 copy-start.3
  3.9 0.7 copy-done.3
  4.5 44.5 %front.1 = (bf16[4,4,16,16,128]{4,3,2,1,0:T(8,128)(2,1)S(1)}, bf16[4,16,32,128]{3,2,1,0:T(8,128)(2,1)S(1)}, bf16[4,16,32,128]{3,2,1,0:T(8,128)(2,1)S(1)}, bf16[4...) custom-call(s32[1,128]{1,0:T(1,128)S(1)} %copy-done.3, s32[1,2048]{1,0:T(1,128)S(1)} %copy-done.2, ...), custom_call_target="tpu_custom_call" | custom-call | tf_op jit(solution)/shard_map/front/pallas_call | solution.py:198
  49.0 7.0 %attend.1 = (bf16[2048,128]{1,0:T(8,128)(2,1)S(1)}, bf16[2048,128]{1,0:T(8,128)(2,1)S(1)}, bf16[4,2,512,128]{3,2,1,0:T(8,128)(2,1)S(1)}) custom-call(bf16[2048,128]{1,0:T(8,128)(2,1)S(1)} %bitcast.8, bf16[2048,128]{1,0:T(8,128)(2,1)S(1)} %bitcast.9, bf16[256,16,128]{2,1,0:T(8,128)(2,1)S(1)} %bitcast.5, s32[4,1,512]{2,1,0:T(1,128)S(1)} %get-tuple-element.19.first), custom_call_target="tpu_custom_call" | custom-call | tf_op jit(solution)/shard_map/attend/pallas_call | solution.py:319
  56.0 76.2 %back.1 = (bf16[128,2048]{1,0:T(8,128)(2,1)S(1)}, bf16[128,2048]{1,0:T(8,128)(2,1)S(1)}, bf16[128,4096]{1,0:T(8,128)(2,1)S(1)}, f32[64,256]{1,0:T(8,128)S(1)}) custom-call(bf16[4,512,128]{2,1,0:T(8,128)(2,1)S(1)} %bitcast.6, bf16[4,512,128]{2,1,0:T(8,128)(2,1)S(1)} %bitcast.7, bf16[4,2,512,128]{3,2,1,0:T(8,128)(2,1)S(1)} %get-tuple-element.22.dkv, ...), custom_call_target="tpu_custom_call" | custom-call | tf_op jit(solution)/shard_map/back/pallas_call | solution.py:560
  132.2 1.4 %store.1 = (bf16[128,2048]{1,0:T(8,128)(2,1)}, bf16[128,2048]{1,0:T(8,128)(2,1)}, bf16[128,4096]{1,0:T(8,128)(2,1)}, f32[64,256]{1,0:T(8,128)}) custom-call(bf16[128,2048]{1,0:T(8,128)(2,1)S(1)} %get-tuple-element.24.a, bf16[128,2048]{1,0:T(8,128)(2,1)S(1)} %get-tuple-element.25.b, bf16[128,4096]{1,0:T(8,128)(2,1)S(1)} %get-tuple-element.26.c, ...), custom_call_target="tpu_custom_call" | custom-call | tf_op jit(solution)/shard_map/store/pallas_call | solution.py:607
  (3 shorter events, 0.0 us)
Async XLA Ops:
  1.1 1.0 copy-start
  2.1 1.0 copy-start.1
  3.2 0.7 copy-start.2
  3.9 0.7 copy-start.3

commit v5 on v4

--- a/solution.py
+++ b/solution.py
@@ -70,12 +70,9 @@
     up, down = {"ctx": (c + 4) % 16}, {"ctx": (c + 12) % 16}
     z_up, z_down = (z + 1) % 4, (z + 3) % 4
 
-    loads = [
-        pltpu.make_async_copy(og_h, og, ls.at[0]),
-        pltpu.make_async_copy(q_h, q, ls.at[1]),
-        pltpu.make_async_copy(x_h, x, ls.at[2]),
-    ]
+    loads = [pltpu.make_async_copy(x_h, x, ls.at[2])]
     loads += [pltpu.make_async_copy(w_h.at[pl.ds(i * 256, 256)], w.at[i], ls.at[3 + i]) for i in range(4)]
+    loads += [pltpu.make_async_copy(og_h, og, ls.at[0]), pltpu.make_async_copy(q_h, q, ls.at[1])]
     for copy in loads:
         copy.start()
     partners = [on_dp(k) for k in range(1, 16)] + [on_y(k) for k in range(1, 4)] + [up, down]
@@ -83,7 +80,14 @@
     for device in partners:
         pl.semaphore_signal(barrier, inc=1, device_id=device, device_id_type=MESH)
 
+    pick = (lax.broadcasted_iota(jnp.int32, (128, 128), 0) == plan[...]).astype(F32).astype(BF)
     loads[0].wait()
+    for j in range(16):
+        sl = slice(j * 256, (j + 1) * 256)
+        t = jnp.dot(pick, x[:, sl], preferred_element_type=F32).astype(BF)
+        xp[:, sl] = t
+        h_s[j % 4, :, (j // 4) * 256 : (j // 4 + 1) * 256] = t
+    loads[5].wait()
     for i in range(8):
         grads = [og[:, h * HD : (h + 1) * HD].astype(F32).reshape(16, 8, HD) for h in (2 * i, 2 * i + 1)]
         g_s[i // 2, :, (i % 2) * 16 : (i % 2 + 1) * 16, :] = jnp.concatenate(grads, 1).astype(BF)
@@ -92,26 +96,8 @@
     for copy in grads:
         copy.start()
 
-    pick = (lax.broadcasted_iota(jnp.int32, (128, 128), 0) == plan[...]).astype(F32).astype(BF)
-    loads[1].wait()
-    for i in range(8):
-        parts = [
-            jnp.dot(pick, q[:, h * HD : (h + 1) * HD], preferred_element_type=F32).reshape(16, 8, HD)
-            for h in (2 * i, 2 * i + 1)
-        ]
-        q_s[:, i * 16 : (i + 1) * 16, :] = jnp.concatenate(parts, 1).astype(BF)
-    q_first = [remote(q_s.at[dp_of[k]], q1.at[d], ss.at[1, k], rs.at[1, k], on_dp(k)) for k in range(1, 16)]
-    for copy in q_first:
-        copy.start()
-
-    loads[2].wait()
-    for j in range(16):
-        sl = slice(j * 256, (j + 1) * 256)
-        t = jnp.dot(pick, x[:, sl], preferred_element_type=F32).astype(BF)
-        xp[:, sl] = t
-        h_s[j % 4, :, (j // 4) * 256 : (j // 4 + 1) * 256] = t
     for i in range(4):
-        loads[3 + i].wait()
+        loads[1 + i].wait()
         acc[i] = rows_dot(xp[...], w[i])
     near_cos, near_sin = turn(cos, sin, pl.ds(y * 16 + d, 1))
     for g in range(4):
@@ -125,30 +111,24 @@
     kv_first = [remote(kv_s.at[dp_of[k]], kv1.at[d], ss.at[0, k], rs.at[0, k], on_dp(k)) for k in range(1, 16)]
     for copy in kv_first:
         copy.start()
+
+    loads[6].wait()
+    for i in range(8):
+        parts = [
+            jnp.dot(pick, q[:, h * HD : (h + 1) * HD], preferred_element_type=F32).reshape(16, 8, HD)
+            for h in (2 * i, 2 * i + 1)
+        ]
+        q_s[:, i * 16 : (i + 1) * 16, :] = jnp.concatenate(parts, 1).astype(BF)
+    q_first = [remote(q_s.at[dp_of[k]], q1.at[d], ss.at[1, k], rs.at[1, k], on_dp(k)) for k in range(1, 16)]
+    for copy in q_first:
+        copy.start()
+    hidden = [remote(h_s.at[y_of[k]], h_rx.at[y], ys.at[3, k], yr.at[3, k], on_y(k)) for k in (1, 3, 2)]
+    hidden[0].start()
+    hidden[1].start()
     kv1[d] = kv_s[d]
     q1[d] = q_s[d]
     g_rx[y] = g_s[y]
     h_rx[y] = h_s[y]
-
-    lane = lax.broadcasted_iota(jnp.int32, (128, 512), 1)
-    take = (lax.broadcasted_iota(jnp.int32, (128, 512), 0) == (lane // 32) * 8 + lane % 8).astype(F32).astype(BF)
-    ids = documents[...].astype(F32)
-    counts = [jnp.sum((ids < k).astype(F32), axis=1, keepdims=True) for k in range(1, 8)]
-    for i in range(4):
-        mine = documents[:, pl.ds(pl.multiple_of(z * 512 + i * 128, 128), 128)].astype(F32)
-        mine = jnp.dot(jnp.broadcast_to(mine, (16, 128)).astype(BF), take, preferred_element_type=F32)[:1]
-        begin = jnp.zeros((1, 512), F32)
-        for k in range(1, 8):
-            begin = jnp.where(mine == k, counts[k - 1], begin)
-        lowest[i] = begin.astype(jnp.int32)
-
-    for copy in q_first:
-        copy.wait_recv()
-    heads = lambda k: pl.ds(pl.multiple_of(y_of[k] * 32, 32), 32)
-    q_second = [remote(q1.at[:, heads(k), :], q_rx.at[y], ys.at[2, k], yr.at[2, k], on_y(k)) for k in range(1, 4)]
-    for copy in q_second:
-        copy.start()
-    q_rx[y] = q1[:, heads(0), :]
 
     for copy in kv_first:
         copy.wait_recv()
@@ -170,9 +150,15 @@
         own_down.append(remote(place, place, zs.at[1, t], zr.at[1, t], down))
         own_up[t].start()
         own_down[t].start()
-    hidden = [remote(h_s.at[y_of[k]], h_rx.at[y], ys.at[3, k], yr.at[3, k], on_y(k)) for k in range(1, 4)]
-    for copy in hidden:
-        copy.start()
+
+    for copy in q_first:
+        copy.wait_recv()
+    heads = lambda k: pl.ds(pl.multiple_of(y_of[k] * 32, 32), 32)
+    q_second = [remote(q1.at[:, heads(k), :], q_rx.at[y], ys.at[2, k], yr.at[2, k], on_y(k)) for k in range(1, 4)]
+    for copy in q_second:
+        copy.start()
+    hidden[2].start()
+    q_rx[y] = q1[:, heads(0), :]
 
     passed = []
     for t in range(4):
@@ -187,6 +173,18 @@
         passed[t].start()
     for t in range(4):
         (own_down if t % 2 == 0 else own_up)[t].wait_recv()
+    lane = lax.broadcasted_iota(jnp.int32, (128, 512), 1)
+    take = (lax.broadcasted_iota(jnp.int32, (128, 512), 0) == (lane // 32) * 8 + lane % 8).astype(F32).astype(BF)
+    ids = documents[...].astype(F32)
+    counts = [jnp.sum((ids < k).astype(F32), axis=1, keepdims=True) for k in range(1, 8)]
+    for i in range(4):
+        mine = documents[:, pl.ds(pl.multiple_of(z * 512 + i * 128, 128), 128)].astype(F32)
+        mine = jnp.dot(jnp.broadcast_to(mine, (16, 128)).astype(BF), take, preferred_element_type=F32)[:1]
+        begin = jnp.zeros((1, 512), F32)
+        for k in range(1, 8):
+            begin = jnp.where(mine == k, counts[k - 1], begin)
+        lowest[i] = begin.astype(jnp.int32)
+
     for copy in passed + q_second + grads + hidden:
         copy.wait_recv()
     for copy in kv_first + grads + q_first + kv_second + own_up + own_down + q_second + hidden + passed:
@@ -384,8 +382,8 @@
             remote(dkv.at[z_down, s, high], fin.at[s, 0, high], zs.at[s, 2], zr.at[s, 2], down),
             remote(dkv.at[z_up, s, low], fin.at[s, 0, low], zs.at[s, 3], zr.at[s, 3], up),
         ]
-        for copy in far[s] + near[s]:
-            copy.start()
+    for copy in far[1] + near[1]:
+        copy.start()
     outs = []
     for i, (a, b) in enumerate(((att, att_rx), (qg, qg_rx))):
         for k in range(1, 4):
@@ -512,8 +510,11 @@
         pieces = [hs[i, :, sl].astype(F32).reshape(16, 8, 256) for i in range(4)]
         hsr[:, sl] = jnp.concatenate(pieces, 1).reshape(512, 256).astype(BF)
     pass_on(1)
+    for copy in far[0] + near[0]:
+        copy.start()
+    complete(1)
     pass_on(0)
-    complete(1)
+    gather(1)
     for copy in outs:
         copy.wait_recv()
     for g in range(4):
@@ -523,9 +524,8 @@
                 cols = slice((g * 4 + h) * HD, (g * 4 + h + 1) * HD)
                 target[:, cols] = block[:, h * 8 : h * 8 + 8, :].reshape(128, HD).astype(BF)
     complete(0)
-    gather(1)
+    multiply(1)
     gather(0)
-    multiply(1)
     add_pair(1)
     multiply(0)
     add_ring(1)

time: 134 us -> 131 us (0.978)
  Pallas kernels: 129 us -> 126 us
    pallas_call x1, Pallas kernels: 76.2 us -> 72.1 us  [back(): pl.pallas_call(back_kernel, in_specs=[vm()] * 6 + [pl.BlockSpec(memory_sp...]
    pallas_call x1, Pallas kernels: 44.5 us -> 46.4 us  [front(): pl.pallas_call(front_kernel, in_specs=[vm()] * 4 + [hbm] * 4, out_specs=[...]
where the time goes in v5:
time: 131 us
  Pallas kernels  126 us (96%)
  local copies, waits for them, and re-layouts  3.43 us (3%)
    pallas_call x1, Pallas kernels, back(): pl.pallas_call(back_kernel, in_specs=[vm()] * 6 + [pl.BlockSpec(memory_sp...  72.1 us
    pallas_call x1, Pallas kernels, front(): pl.pallas_call(front_kernel, in_specs=[vm()] * 4 + [hbm] * 4, out_specs=[...  46.4 us
    pallas_call x1, Pallas kernels, attend(): pl.pallas_call(attend_kernel, in_specs=[vm()] * 4, out_specs=[vm()] * 3,...  6.15 us
    unnamed x8, local copies, waits for them, and re-layouts  3.43 us

profile of v5, /device:TPU:1, one launch (start us, length us, event | category | flops | bytes accessed | tf_op | source)
XLA Modules:
  0.0 130.6 jit_solution(5382736392107642385)
XLA Ops:
  0.7 0.1 add_convert_fusion
  0.8 0.2 fusion
  1.0 0.1 pad_maximum_fusion
  1.1 0.0 copy-start
  1.1 1.0 copy-done
  2.1 0.0 copy-start.1
  2.1 1.0 copy-done.1
  3.2 0.0 copy-start.2
  3.2 0.7 copy-done.2
  3.9 0.0 copy-start.3
  3.9 0.7 copy-done.3
  4.5 46.4 %front.1 = (bf16[4,4,16,16,128]{4,3,2,1,0:T(8,128)(2,1)S(1)}, bf16[4,16,32,128]{3,2,1,0:T(8,128)(2,1)S(1)}, bf16[4,16,32,128]{3,2,1,0:T(8,128)(2,1)S(1)}, bf16[4...) custom-call(s32[1,128]{1,0:T(1,128)S(1)} %copy-done.3, s32[1,2048]{1,0:T(1,128)S(1)} %copy-done.2, ...), custom_call_target="tpu_custom_call" | custom-call | tf_op jit(solution)/shard_map/front/pallas_call | solution.py:196
  50.9 6.2 %attend.1 = (bf16[2048,128]{1,0:T(8,128)(2,1)S(1)}, bf16[2048,128]{1,0:T(8,128)(2,1)S(1)}, bf16[4,2,512,128]{3,2,1,0:T(8,128)(2,1)S(1)}) custom-call(bf16[2048,128]{1,0:T(8,128)(2,1)S(1)} %bitcast.8, bf16[2048,128]{1,0:T(8,128)(2,1)S(1)} %bitcast.9, bf16[256,16,128]{2,1,0:T(8,128)(2,1)S(1)} %bitcast.5, s32[4,1,512]{2,1,0:T(1,128)S(1)} %get-tuple-element.19.first), custom_call_target="tpu_custom_call" | custom-call | tf_op jit(solution)/shard_map/attend/pallas_call | solution.py:317
  57.1 72.1 %back.1 = (bf16[128,2048]{1,0:T(8,128)(2,1)S(1)}, bf16[128,2048]{1,0:T(8,128)(2,1)S(1)}, bf16[128,4096]{1,0:T(8,128)(2,1)S(1)}, f32[64,256]{1,0:T(8,128)S(1)}) custom-call(bf16[4,512,128]{2,1,0:T(8,128)(2,1)S(1)} %bitcast.6, bf16[4,512,128]{2,1,0:T(8,128)(2,1)S(1)} %bitcast.7, bf16[4,2,512,128]{3,2,1,0:T(8,128)(2,1)S(1)} %get-tuple-element.22.dkv, ...), custom_call_target="tpu_custom_call" | custom-call | tf_op jit(solution)/shard_map/back/pallas_call | solution.py:560
  129.2 1.4 %store.1 = (bf16[128,2048]{1,0:T(8,128)(2,1)}, bf16[128,2048]{1,0:T(8,128)(2,1)}, bf16[128,4096]{1,0:T(8,128)(2,1)}, f32[64,256]{1,0:T(8,128)}) custom-call(bf16[128,2048]{1,0:T(8,128)(2,1)S(1)} %get-tuple-element.24.a, bf16[128,2048]{1,0:T(8,128)(2,1)S(1)} %get-tuple-element.25.b, bf16[128,4096]{1,0:T(8,128)(2,1)S(1)} %get-tuple-element.26.c, ...), custom_call_target="tpu_custom_call" | custom-call | tf_op jit(solution)/shard_map/store/pallas_call | solution.py:607
  (3 shorter events, 0.0 us)
Async XLA Ops:
  1.1 1.0 copy-start
  2.1 1.0 copy-start.1
  3.2 0.7 copy-start.2
  3.9 0.7 copy-start.3

commit v6 on v5

--- a/solution.py
+++ b/solution.py
@@ -15,7 +15,6 @@
 BF = jnp.bfloat16
 F32 = jnp.float32
 MESH = pl.DeviceIdType.MESH
-KB = 256
 MIB = 1024 * 1024
 
 
@@ -255,29 +254,42 @@
         og_t[...] = og[here, :].astype(F32).T.astype(BF)
         lowest = first[qb]
         start = (jnp.min(lowest) // 128) * 128
-        count = (base + (qb + 1) * 128 - start + KB - 1) // KB
+        span = base + (qb + 1) * 128 - start
+        blocks = []
+        for size in (1024, 512, 256, 128):
+            count = (span + 128) // size if size == 512 else span // size
+            blocks.append((size, count))
+            span = jnp.maximum(span - size * count, 0)
+
+        def sweep(part, carry):
+            first_row = start
+            for size, count in blocks:
+                carry = lax.fori_loop(0, count, functools.partial(part, size, first_row), carry)
+                first_row = first_row + size * count
+            return carry
+
         lane = lax.broadcasted_iota(jnp.int32, (1, 512), 1)
         position = base + qb * 128 + (lane // 32) * 8 + lane % 8
         out_t[...] = jnp.zeros_like(out_t)
         grad_t[...] = jnp.zeros_like(grad_t)
 
         def eights(t):
-            return t.reshape(KB // 8, 8, 512)
-
-        def scores(i, top):
-            at = pl.multiple_of(start + i * KB, 128)
-            rows = pl.ds(at, KB)
+            return t.reshape(t.shape[0] // 8, 8, 512)
+
+        def scores(size, at, i, top):
+            at = pl.multiple_of(at + i * size, 128)
+            rows = pl.ds(at, size)
             s = jnp.dot(keys[rows, :], q_t[...], preferred_element_type=F32)
-            index = at + lax.broadcasted_iota(jnp.int32, (KB, 512), 0)
+            index = at + lax.broadcasted_iota(jnp.int32, (size, 512), 0)
             s = jnp.where((index <= position) & (index >= lowest), s, MASK_VALUE)
             sc[rows, :] = s
             return jnp.maximum(top, jnp.max(eights(s), axis=0))
 
-        top = lax.fori_loop(0, count, scores, jnp.full((8, 512), MASK_VALUE, F32))
+        top = sweep(scores, jnp.full((8, 512), MASK_VALUE, F32))
         top = jnp.max(top, axis=0, keepdims=True) * fold
 
-        def expo(i, sums):
-            rows = pl.ds(pl.multiple_of(start + i * KB, 128), KB)
+        def expo(size, at, i, sums):
+            rows = pl.ds(pl.multiple_of(at + i * size, 128), size)
             e = jnp.exp2(sc[rows, :] * fold - top)
             grad = jnp.dot(vals[rows, :], og_t[...], preferred_element_type=F32)
             sc[rows, :] = e
@@ -285,13 +297,12 @@
             return sums[0] + jnp.sum(eights(e), axis=0), sums[1] + jnp.sum(eights(e * grad), axis=0)
 
         zero = jnp.zeros((8, 512), F32)
-        total, product = lax.fori_loop(0, count, expo, (zero, zero))
+        total, product = sweep(expo, (zero, zero))
         inverse = 1.0 / jnp.sum(total, axis=0, keepdims=True)
         delta = jnp.sum(product, axis=0, keepdims=True) * inverse
 
-        def both(i, c):
-            at = pl.multiple_of(start + i * KB, 128)
-            rows = pl.ds(at, KB)
+        def both(size, at, i, c):
+            rows = pl.ds(pl.multiple_of(at + i * size, 128), size)
             p = sc[rows, :] * inverse
             rounded = p.astype(BF)
             ds = (p * (gp[rows, :] - delta)).astype(BF)
@@ -301,7 +312,7 @@
             grad_t[...] += jnp.dot(keys_t[:, rows], ds, preferred_element_type=F32)
             return c
 
-        lax.fori_loop(0, count, both, 0)
+        sweep(both, 0)
         att[here, :] = out_t[...].T.astype(BF)
         qg[here, :] = (grad_t[...] * SCALE).T.astype(BF)
         return carry
@@ -460,9 +471,7 @@
         for k in order:
             g = x_of[k]
             rows = src[s, g].reshape(512, HD)
-            for j in range(4):
-                sl = slice(j * 256, (j + 1) * 256)
-                tile[s, k, :, :, sl] = cols_dot(rows, hsr[:, sl]).reshape(2, 64, 256).astype(BF)
+            tile[s, k] = cols_dot(rows, hsr[...]).reshape(2, 64, 1024).astype(BF)
             copy = remote(tile.at[s, k, 1 - core], pair.at[s, k], cs.at[s, k], cr.at[s, k], sibling)
             copy.start()
             swaps[s].append(copy)

time: 131 us -> 125 us (0.954)
  Pallas kernels: 126 us -> 120 us
    pallas_call x1, Pallas kernels: 72.1 us -> 67 us  [back(): pl.pallas_call(back_kernel, in_specs=[vm()] * 6 + [pl.BlockSpec(memory_sp...]
where the time goes in v6:
time: 125 us
  Pallas kernels  120 us (96%)
  local copies, waits for them, and re-layouts  3.43 us (3%)
    pallas_call x1, Pallas kernels, back(): pl.pallas_call(back_kernel, in_specs=[vm()] * 6 + [pl.BlockSpec(memory_sp...  67 us
    pallas_call x1, Pallas kernels, front(): pl.pallas_call(front_kernel, in_specs=[vm()] * 4 + [hbm] * 4, out_specs=[...  46.6 us
    pallas_call x1, Pallas kernels, attend(): pl.pallas_call(attend_kernel, in_specs=[vm()] * 4, out_specs=[vm()] * 3,...  5.56 us
    unnamed x8, local copies, waits for them, and re-layouts  3.43 us

profile of v6, /device:TPU:1, one launch (start us, length us, event | category | flops | bytes accessed | tf_op | source)
XLA Modules:
  0.0 125.2 jit_solution(15344551148380005595)
XLA Ops:
  0.7 0.1 add_convert_fusion
  0.8 0.2 fusion
  1.0 0.1 pad_maximum_fusion
  1.1 0.0 copy-start
  1.1 1.0 copy-done
  2.1 0.0 copy-start.1
  2.1 1.0 copy-done.1
  3.2 0.0 copy-start.2
  3.2 0.7 copy-done.2
  3.9 0.0 copy-start.3
  3.9 0.7 copy-done.3
  4.5 46.6 %front.1 = (bf16[4,4,16,16,128]{4,3,2,1,0:T(8,128)(2,1)S(1)}, bf16[4,16,32,128]{3,2,1,0:T(8,128)(2,1)S(1)}, bf16[4,16,32,128]{3,2,1,0:T(8,128)(2,1)S(1)}, bf16[4...) custom-call(s32[1,128]{1,0:T(1,128)S(1)} %copy-done.3, s32[1,2048]{1,0:T(1,128)S(1)} %copy-done.2, ...), custom_call_target="tpu_custom_call" | custom-call | tf_op jit(solution)/shard_map/front/pallas_call | solution.py:195
  51.1 5.6 %attend.1 = (bf16[2048,128]{1,0:T(8,128)(2,1)S(1)}, bf16[2048,128]{1,0:T(8,128)(2,1)S(1)}, bf16[4,2,512,128]{3,2,1,0:T(8,128)(2,1)S(1)}) custom-call(bf16[2048,128]{1,0:T(8,128)(2,1)S(1)} %bitcast.8, bf16[2048,128]{1,0:T(8,128)(2,1)S(1)} %bitcast.9, bf16[256,16,128]{2,1,0:T(8,128)(2,1)S(1)} %bitcast.5, s32[4,1,512]{2,1,0:T(1,128)S(1)} %get-tuple-element.19.first), custom_call_target="tpu_custom_call" | custom-call | tf_op jit(solution)/shard_map/attend/pallas_call | solution.py:328
  56.6 67.0 %back.1 = (bf16[128,2048]{1,0:T(8,128)(2,1)S(1)}, bf16[128,2048]{1,0:T(8,128)(2,1)S(1)}, bf16[128,4096]{1,0:T(8,128)(2,1)S(1)}, f32[64,256]{1,0:T(8,128)S(1)}) custom-call(bf16[4,512,128]{2,1,0:T(8,128)(2,1)S(1)} %bitcast.6, bf16[4,512,128]{2,1,0:T(8,128)(2,1)S(1)} %bitcast.7, bf16[4,2,512,128]{3,2,1,0:T(8,128)(2,1)S(1)} %get-tuple-element.22.dkv, ...), custom_call_target="tpu_custom_call" | custom-call | tf_op jit(solution)/shard_map/back/pallas_call | solution.py:569
  123.7 1.4 %store.1 = (bf16[128,2048]{1,0:T(8,128)(2,1)}, bf16[128,2048]{1,0:T(8,128)(2,1)}, bf16[128,4096]{1,0:T(8,128)(2,1)}, f32[64,256]{1,0:T(8,128)}) custom-call(bf16[128,2048]{1,0:T(8,128)(2,1)S(1)} %get-tuple-element.24.a, bf16[128,2048]{1,0:T(8,128)(2,1)S(1)} %get-tuple-element.25.b, bf16[128,4096]{1,0:T(8,128)(2,1)S(1)} %get-tuple-element.26.c, ...), custom_call_target="tpu_custom_call" | custom-call | tf_op jit(solution)/shard_map/store/pallas_call | solution.py:616
  (3 shorter events, 0.0 us)
Async XLA Ops:
  1.1 1.0 copy-start
  2.1 1.0 copy-start.1
  3.2 0.7 copy-start.2
  3.9 0.7 copy-start.3

commit v7 on v6

--- a/solution.py
+++ b/solution.py
@@ -57,7 +57,7 @@
 
 
 def front_kernel(
-    plan, documents, cos, sin, x_h, q_h, og_h, w_h, kv_all, q_rx, g_rx, h_rx, lowest,
+    plan_ids, cos, sin, x_h, q_h, og_h, w_h, kv_all, q_rx, g_rx, h_rx, lowest,
     x, q, og, w, xp, acc, kv_s, q_s, g_s, h_s, kv1, q1, ls, ss, rs, ys, yr, zs, zr,
 ):
     d, c = lax.axis_index("dp"), lax.axis_index("ctx")
@@ -79,7 +79,7 @@
     for device in partners:
         pl.semaphore_signal(barrier, inc=1, device_id=device, device_id_type=MESH)
 
-    pick = (lax.broadcasted_iota(jnp.int32, (128, 128), 0) == plan[...]).astype(F32).astype(BF)
+    pick = (lax.broadcasted_iota(jnp.int32, (128, 128), 0) == plan_ids[:, :128]).astype(F32).astype(BF)
     loads[0].wait()
     for j in range(16):
         sl = slice(j * 256, (j + 1) * 256)
@@ -174,10 +174,10 @@
         (own_down if t % 2 == 0 else own_up)[t].wait_recv()
     lane = lax.broadcasted_iota(jnp.int32, (128, 512), 1)
     take = (lax.broadcasted_iota(jnp.int32, (128, 512), 0) == (lane // 32) * 8 + lane % 8).astype(F32).astype(BF)
-    ids = documents[...].astype(F32)
+    ids = plan_ids[:, 128:].astype(F32)
     counts = [jnp.sum((ids < k).astype(F32), axis=1, keepdims=True) for k in range(1, 8)]
     for i in range(4):
-        mine = documents[:, pl.ds(pl.multiple_of(z * 512 + i * 128, 128), 128)].astype(F32)
+        mine = plan_ids[:, pl.ds(pl.multiple_of(z * 512 + (i + 1) * 128, 128), 128)].astype(F32)
         mine = jnp.dot(jnp.broadcast_to(mine, (16, 128)).astype(BF), take, preferred_element_type=F32)[:1]
         begin = jnp.zeros((1, 512), F32)
         for k in range(1, 8):
@@ -190,11 +190,11 @@
         copy.wait_send()
 
 
-def front(plan, documents, cos, sin, x, q, og, w):
+def front(plan_ids, cos, sin, x, q, og, w):
     hbm = pl.BlockSpec(memory_space=pltpu.HBM)
     return pl.pallas_call(
         front_kernel,
-        in_specs=[vm()] * 4 + [hbm] * 4,
+        in_specs=[vm()] * 3 + [hbm] * 4,
         out_specs=[vm()] * 5,
         out_shape=[
             jax.ShapeDtypeStruct((4, 4, 16, 16, HD), BF),
@@ -226,10 +226,10 @@
         ],
         compiler_params=pltpu.CompilerParams(collective_id=0, has_side_effects=True, vmem_limit_bytes=49 * MIB),
         name="front",
-    )(plan, documents, cos, sin, x, q, og, w)
-
-
-def attend_kernel(q, og, kv, first, att, qg, dkv, keys, vals, keys_t, vals_t, dk, dv, sc, gp, q_t, og_t, out_t, grad_t):
+    )(plan_ids, cos, sin, x, q, og, w)
+
+
+def attend_kernel(q, og, kv, first, att, qg, dkv, keys, vals, keys_t, vals_t, dk, dv, sc, gp, q_t, og_t, out_t, grad_t, tops):
     base = (lax.axis_index("ctx") // 4) * 512
     for i in range(4):
         block = kv[pl.ds(i * 64, 64)].astype(F32)
@@ -276,34 +276,35 @@
         def eights(t):
             return t.reshape(t.shape[0] // 8, 8, 512)
 
-        def scores(size, at, i, top):
+        def scores(size, at, i, sums):
             at = pl.multiple_of(at + i * size, 128)
             rows = pl.ds(at, size)
             s = jnp.dot(keys[rows, :], q_t[...], preferred_element_type=F32)
+            grad = jnp.dot(vals[rows, :], og_t[...], preferred_element_type=F32)
+            gp[rows, :] = grad
             index = at + lax.broadcasted_iota(jnp.int32, (size, 512), 0)
             s = jnp.where((index <= position) & (index >= lowest), s, MASK_VALUE)
-            sc[rows, :] = s
-            return jnp.maximum(top, jnp.max(eights(s), axis=0))
-
-        top = sweep(scores, jnp.full((8, 512), MASK_VALUE, F32))
-        top = jnp.max(top, axis=0, keepdims=True) * fold
-
-        def expo(size, at, i, sums):
-            rows = pl.ds(pl.multiple_of(at + i * size, 128), size)
-            e = jnp.exp2(sc[rows, :] * fold - top)
-            grad = jnp.dot(vals[rows, :], og_t[...], preferred_element_type=F32)
+            top, total, product = sums
+            high = jnp.maximum(top, jnp.max(jnp.max(eights(s), axis=0), axis=0, keepdims=True) * fold)
+            e = jnp.exp2(s * fold - high)
             sc[rows, :] = e
-            gp[rows, :] = grad
-            return sums[0] + jnp.sum(eights(e), axis=0), sums[1] + jnp.sum(eights(e * grad), axis=0)
+            tops[at // 128] = high
+            shrink = jnp.exp2(top - high)
+            return (
+                high,
+                total * shrink + jnp.sum(eights(e), axis=0),
+                product * shrink + jnp.sum(eights(e * grad), axis=0),
+            )
 
         zero = jnp.zeros((8, 512), F32)
-        total, product = sweep(expo, (zero, zero))
+        top, total, product = sweep(scores, (jnp.full((1, 512), MASK_VALUE, F32), zero, zero))
         inverse = 1.0 / jnp.sum(total, axis=0, keepdims=True)
         delta = jnp.sum(product, axis=0, keepdims=True) * inverse
 
         def both(size, at, i, c):
-            rows = pl.ds(pl.multiple_of(at + i * size, 128), size)
-            p = sc[rows, :] * inverse
+            at = pl.multiple_of(at + i * size, 128)
+            rows = pl.ds(at, size)
+            p = sc[rows, :] * (jnp.exp2(tops[at // 128] - top) * inverse)
             rounded = p.astype(BF)
             ds = (p * (gp[rows, :] - delta)).astype(BF)
             dv[rows, :] += jnp.dot(rounded, og[here, :], preferred_element_type=F32)
@@ -342,6 +343,7 @@
             pltpu.VMEM((HD, 512), BF),
             pltpu.VMEM((HD, 512), F32),
             pltpu.VMEM((HD, 512), F32),
+            pltpu.VMEM((17, 1, 512), F32),
         ],
         out_shape=[
             jax.ShapeDtypeStruct((2048, HD), BF),
@@ -465,26 +467,29 @@
     swaps = {0: [], 1: []}
     order = [2, 1, 3, 0]
 
+    swap = lambda s, g: remote(tile.at[s, g, 1 - core], pair.at[s, g], cs.at[s, g], cr.at[s, g], sibling)
+
     def multiply(s):
-        for copy in gathered[s]:
-            copy.wait_recv()
+        for k in (0, 1, 3, 2):
+            if k:
+                gathered[s][k - 1].wait_recv()
+            g = y_of[(4 - k) % 4]
+            rows = src[s, g].reshape(512, HD)
+            tile[s, g] = cols_dot(rows, hsr[...]).reshape(2, 64, 1024).astype(BF)
+            copy = swap(s, g)
+            copy.start()
+            swaps[s].append(copy)
+
+    rings = {0: [], 1: []}
+
+    def add_pair(s):
         for k in order:
             g = x_of[k]
-            rows = src[s, g].reshape(512, HD)
-            tile[s, k] = cols_dot(rows, hsr[...]).reshape(2, 64, 1024).astype(BF)
-            copy = remote(tile.at[s, k, 1 - core], pair.at[s, k], cs.at[s, k], cr.at[s, k], sibling)
-            copy.start()
-            swaps[s].append(copy)
-
-    rings = {0: [], 1: []}
-
-    def add_pair(s):
-        for copy, k in zip(swaps[s], order):
-            copy.wait_recv()
+            swap(s, g).wait_recv()
             for j in range(4):
                 sl = slice(j * 256, (j + 1) * 256)
                 mine[s, k, :, sl] = (
-                    tile[s, k, core, :, sl].astype(F32) + pair[s, k, :, sl].astype(F32)
+                    tile[s, g, core, :, sl].astype(F32) + pair[s, g, :, sl].astype(F32)
                 ).astype(BF)
             if k:
                 copy = remote(mine.at[s, k], ring.at[s, k], xs.at[s, k], xr.at[s, k], on_x(k))
@@ -628,9 +633,8 @@
     z = lax.axis_index("ctx") // 4
     small = jnp.arange(8, dtype=jnp.int32)
     cos, sin = angle_tables(jnp.concatenate([z * 512 + jnp.arange(64, dtype=jnp.int32) * 8, small]))
-    kv_all, q_rx, g_rx, h_rx, first = front(
-        packing_plan, document_ids, cos, sin, hidden_rows, query_rows, out_grad, projection
-    )
+    plan_ids = jnp.concatenate([packing_plan, document_ids], axis=1)
+    kv_all, q_rx, g_rx, h_rx, first = front(plan_ids, cos, sin, hidden_rows, query_rows, out_grad, projection)
     att, qg, dkv = attend(
         q_rx.reshape(2048, HD), g_rx.reshape(2048, HD), kv_all.reshape(256, 16, HD), first
     )

time: 125 us -> 123 us (0.984)
  local copies, waits for them, and re-layouts: 3.43 us -> 2.08 us
    unnamed x8 -> x4, local copies, waits for them, and re-layouts: 3.43 us -> 2.08 us
where the time goes in v7:
time: 123 us; the launch traced here: 124 us
  Pallas kernels  120 us (98%)
  local copies, waits for them, and re-layouts  2.08 us (2%)
    pallas_call x1, Pallas kernels, back(): pl.pallas_call(back_kernel, in_specs=[vm()] * 6 + [pl.BlockSpec(memory_sp...  66.6 us
    pallas_call x1, Pallas kernels, front(): pl.pallas_call(front_kernel, in_specs=[vm()] * 3 + [hbm] * 4, out_specs=[...  46.5 us
    pallas_call x1, Pallas kernels, attend(): pl.pallas_call(attend_kernel, in_specs=[vm()] * 4, out_specs=[vm()] * 3,...  5.22 us

profile of v7, /device:TPU:1, one launch (start us, length us, event | category | flops | bytes accessed | tf_op | source)
XLA Modules:
  0.0 123.7 jit_solution(6498089394265816229)
XLA Ops:
  0.7 0.1 add_convert_fusion
  0.8 0.7 pad_add_fusion.plan_ids
  1.5 0.2 fusion
  1.7 0.1 pad_maximum_fusion
  1.8 0.0 copy-start
  1.8 1.0 copy-done
  2.8 0.0 copy-start.1
  2.8 1.0 copy-done.1
  3.9 46.5 %front.1 = (bf16[4,4,16,16,128]{4,3,2,1,0:T(8,128)(2,1)S(1)}, bf16[4,16,32,128]{3,2,1,0:T(8,128)(2,1)S(1)}, bf16[4,16,32,128]{3,2,1,0:T(8,128)(2,1)S(1)}, bf16[4...) custom-call(s32[1,2176]{1,0:T(1,128)S(1)} %pad_add_fusion.plan_ids, f32[72,128]{1,0:T(8,128)S(1)} %get-tuple-element.31.cos, ...), custom_call_target="tpu_custom_call" | custom-call | tf_op jit(solution)/shard_map/front/pallas_call | solution.py:195
  50.3 5.2 %attend.1 = (bf16[2048,128]{1,0:T(8,128)(2,1)S(1)}, bf16[2048,128]{1,0:T(8,128)(2,1)S(1)}, bf16[4,2,512,128]{3,2,1,0:T(8,128)(2,1)S(1)}) custom-call(bf16[2048,128]{1,0:T(8,128)(2,1)S(1)} %bitcast.8, bf16[2048,128]{1,0:T(8,128)(2,1)S(1)} %bitcast.9, bf16[256,16,128]{2,1,0:T(8,128)(2,1)S(1)} %bitcast.5, s32[4,1,512]{2,1,0:T(1,128)S(1)} %get-tuple-element.19.first), custom_call_target="tpu_custom_call" | custom-call | tf_op jit(solution)/shard_map/attend/pallas_call | solution.py:329
  55.6 66.6 %back.1 = (bf16[128,2048]{1,0:T(8,128)(2,1)S(1)}, bf16[128,2048]{1,0:T(8,128)(2,1)S(1)}, bf16[128,4096]{1,0:T(8,128)(2,1)S(1)}, f32[64,256]{1,0:T(8,128)S(1)}) custom-call(bf16[4,512,128]{2,1,0:T(8,128)(2,1)S(1)} %bitcast.6, bf16[4,512,128]{2,1,0:T(8,128)(2,1)S(1)} %bitcast.7, bf16[4,2,512,128]{3,2,1,0:T(8,128)(2,1)S(1)} %get-tuple-element.22.dkv, ...), custom_call_target="tpu_custom_call" | custom-call | tf_op jit(solution)/shard_map/back/pallas_call | solution.py:574
  122.1 1.4 %store.1 = (bf16[128,2048]{1,0:T(8,128)(2,1)}, bf16[128,2048]{1,0:T(8,128)(2,1)}, bf16[128,4096]{1,0:T(8,128)(2,1)}, f32[64,256]{1,0:T(8,128)}) custom-call(bf16[128,2048]{1,0:T(8,128)(2,1)S(1)} %get-tuple-element.24.a, bf16[128,2048]{1,0:T(8,128)(2,1)S(1)} %get-tuple-element.25.b, bf16[128,4096]{1,0:T(8,128)(2,1)S(1)} %get-tuple-element.26.c, ...), custom_call_target="tpu_custom_call" | custom-call | tf_op jit(solution)/shard_map/store/pallas_call | solution.py:621
  (3 shorter events, 0.0 us)
Async XLA Ops:
  1.8 1.0 copy-start
  2.8 1.0 copy-start.1

commit v8 on v7

--- a/solution.py
+++ b/solution.py
@@ -633,6 +633,9 @@
     z = lax.axis_index("ctx") // 4
     small = jnp.arange(8, dtype=jnp.int32)
     cos, sin = angle_tables(jnp.concatenate([z * 512 + jnp.arange(64, dtype=jnp.int32) * 8, small]))
+    hidden_rows, query_rows, out_grad = [
+        pltpu.with_memory_space_constraint(a, pltpu.HBM) for a in (hidden_rows, query_rows, out_grad)
+    ]
     plan_ids = jnp.concatenate([packing_plan, document_ids], axis=1)
     kv_all, q_rx, g_rx, h_rx, first = front(plan_ids, cos, sin, hidden_rows, query_rows, out_grad, projection)
     att, qg, dkv = attend(

time: 123 us -> 125 us (1.016)
  Pallas kernels: 120 us -> 124 us
  local copies, waits for them, and re-layouts: 2.08 us -> 0.01 us
    unnamed x4 -> x0, local copies, waits for them, and re-layouts: 2.08 us -> none
    pallas_call x1, Pallas kernels: 66.6 us -> 68.5 us  [back(): pl.pallas_call(back_kernel, in_specs=[vm()] * 6 + [pl.BlockSpec(memory_sp...]
    pallas_call x1, Pallas kernels: 46.5 us -> 48.4 us  [front(): pl.pallas_call(front_kernel, in_specs=[vm()] * 3 + [hbm] * 4, out_specs=[...]
where the time goes in v8:
time: 125 us; the launch traced here: 126 us
  Pallas kernels  124 us (99%)
    pallas_call x1, Pallas kernels, back(): pl.pallas_call(back_kernel, in_specs=[vm()] * 6 + [pl.BlockSpec(memory_sp...  68.5 us
    pallas_call x1, Pallas kernels, front(): pl.pallas_call(front_kernel, in_specs=[vm()] * 3 + [hbm] * 4, out_specs=[...  48.4 us
    pallas_call x1, Pallas kernels, attend(): pl.pallas_call(attend_kernel, in_specs=[vm()] * 4, out_specs=[vm()] * 3,...  6.03 us

profile of v8, /device:TPU:1, one launch (start us, length us, event | category | flops | bytes accessed | tf_op | source)
XLA Modules:
  0.0 126.2 jit_solution(11641720432185603900)
XLA Ops:
  0.7 0.1 add_convert_fusion
  0.8 0.7 pad_add_fusion.plan_ids
  1.5 0.2 fusion
  1.7 0.1 pad_maximum_fusion
  1.8 48.4 %front.1 = (bf16[4,4,16,16,128]{4,3,2,1,0:T(8,128)(2,1)S(1)}, bf16[4,16,32,128]{3,2,1,0:T(8,128)(2,1)S(1)}, bf16[4,16,32,128]{3,2,1,0:T(8,128)(2,1)S(1)}, bf16[4...) custom-call(s32[1,2176]{1,0:T(1,128)S(1)} %pad_add_fusion.plan_ids, f32[72,128]{1,0:T(8,128)S(1)} %get-tuple-element.31.cos, ...), custom_call_target="tpu_custom_call" | custom-call | tf_op jit(solution)/shard_map/front/pallas_call | solution.py:195
  50.1 6.0 %attend.1 = (bf16[2048,128]{1,0:T(8,128)(2,1)S(1)}, bf16[2048,128]{1,0:T(8,128)(2,1)S(1)}, bf16[4,2,512,128]{3,2,1,0:T(8,128)(2,1)S(1)}) custom-call(bf16[2048,128]{1,0:T(8,128)(2,1)S(1)} %bitcast.8, bf16[2048,128]{1,0:T(8,128)(2,1)S(1)} %bitcast.9, bf16[256,16,128]{2,1,0:T(8,128)(2,1)S(1)} %bitcast.5, s32[4,1,512]{2,1,0:T(1,128)S(1)} %get-tuple-element.19.first), custom_call_target="tpu_custom_call" | custom-call | tf_op jit(solution)/shard_map/attend/pallas_call | solution.py:329
  56.2 68.5 %back.1 = (bf16[128,2048]{1,0:T(8,128)(2,1)S(1)}, bf16[128,2048]{1,0:T(8,128)(2,1)S(1)}, bf16[128,4096]{1,0:T(8,128)(2,1)S(1)}, f32[64,256]{1,0:T(8,128)S(1)}) custom-call(bf16[4,512,128]{2,1,0:T(8,128)(2,1)S(1)} %bitcast.6, bf16[4,512,128]{2,1,0:T(8,128)(2,1)S(1)} %bitcast.7, bf16[4,2,512,128]{3,2,1,0:T(8,128)(2,1)S(1)} %get-tuple-element.22.dkv, ...), custom_call_target="tpu_custom_call" | custom-call | tf_op jit(solution)/shard_map/back/pallas_call | solution.py:574
  124.7 1.4 %store.1 = (bf16[128,2048]{1,0:T(8,128)(2,1)}, bf16[128,2048]{1,0:T(8,128)(2,1)}, bf16[128,4096]{1,0:T(8,128)(2,1)}, f32[64,256]{1,0:T(8,128)}) custom-call(bf16[128,2048]{1,0:T(8,128)(2,1)S(1)} %get-tuple-element.24.a, bf16[128,2048]{1,0:T(8,128)(2,1)S(1)} %get-tuple-element.25.b, bf16[128,4096]{1,0:T(8,128)(2,1)S(1)} %get-tuple-element.26.c, ...), custom_call_target="tpu_custom_call" | custom-call | tf_op jit(solution)/shard_map/store/pallas_call | solution.py:621
  (3 shorter events, 0.0 us)
